TPU v7x, 32 devices: a whole 2x2x4 slice. The times are simulated.
32 devices in a mesh: dp: 8 (over y, x, core), vocab: 4 (over z).
Axes of the slice: x: 2, y: 2, z: 4, core: 2. Of those that a mesh axis runs over, the one named last changes fastest.
Arguments:
- hidden_in: bfloat16 [256, 3584], P(None, 'dp'), may hold values from -64 to 64
- pre_gain: float32 [3584], P('dp'), may hold values from 0.1 to 1.9
- gate_weight: bfloat16 [3584, 14336], P('dp', 'vocab'), may hold values from -0.09375 to 0.09375
- up_weight: bfloat16 [3584, 14336], P('dp', 'vocab'), may hold values from -0.09375 to 0.09375
- down_weight: bfloat16 [14336, 3584], P('vocab', 'dp'), may hold values from -0.046875 to 0.046875
- post_gain: float32 [3584], P('dp'), may hold values from 0.1 to 1.9
- final_gain: float32 [3584], P('dp'), may hold values from 0.1 to 1.9
- embedding: bfloat16 [8192, 3584], P(('dp', 'vocab')), may hold values from -0.3984375 to 0.3984375
- teacher_logits: bfloat16 [256, 8192], P('vocab', 'dp'), may hold values from -30 to 30
- target_ids: int32 [256], replicated, may hold values from 0 to 8191
- lengths: int32 [2], replicated, may hold values from 32 to 128, as said below
Outputs:
- loss: float32 [], replicated
- grad_hidden: bfloat16 [256, 3584], P(None, 'dp')
- grad_gate: bfloat16 [3584, 14336], P('dp', 'vocab')
- grad_up: bfloat16 [3584, 14336], P('dp', 'vocab')
- grad_down: bfloat16 [14336, 3584], P('vocab', 'dp')
- grad_embedding: bfloat16 [8192, 3584], P(('dp', 'vocab'))
Inputs may be any that keep to these rules, and one draw needn't show every extreme that they name: The first lengths[k] positions of sequence k are tokens, the rest padding; some sequence has all 128.
All inputs are finite; a program needn't handle non-finite values.
Results may differ from a plain program's by a relative error of at most 0.015.
Values may be sent and summed in bfloat16 or wider, within the bound.
A program may use at most 128 MiB of HBM per device.

v0:
```python
import jax
import jax.numpy as jnp
from jax import lax
from jax.sharding import PartitionSpec as P

D = 3584
LENGTH = 128


eps = 1e-06
softcap_value = 30.0
hard_weight = 0.5
loss_scale = 131072.0


def gelu_tanh(value):
    return jax.nn.gelu(value, approximate=True)


def token_mask(lengths, count):
    positions = jnp.arange(count, dtype=jnp.int32)
    sequence = positions // LENGTH
    within = positions % LENGTH
    match = sequence[:, None] == jnp.arange(lengths.shape[0], dtype=jnp.int32)[None, :]
    limit = jnp.sum(jnp.where(match, lengths[None, :], 0), axis=1)
    return jnp.where(within < limit, 1.0, 0.0).astype(jnp.float32)


def contract_last(left, right):
    return lax.dot_general(
        left, right, (((1,), (1,)), ((), ())), preferred_element_type=jnp.float32
    )


def contract_first(left, right):
    return lax.dot_general(
        left, right, (((0,), (0,)), ((), ())), preferred_element_type=jnp.float32
    )


def on_device(
    hidden_in,
    pre_gain,
    gate_weight,
    up_weight,
    down_weight,
    post_gain,
    final_gain,
    embedding,
    teacher_logits,
    target_ids,
    lengths,
):
    positions = hidden_in.shape[0]
    xf = hidden_in.astype(jnp.float32)
    square_in = lax.psum(jnp.sum(xf * xf, axis=1), "dp")
    rms_in = lax.rsqrt(square_in / D + eps)[:, None]
    z = (xf * rms_in * pre_gain).astype(jnp.bfloat16)
    gate_terms = jnp.dot(z, gate_weight, preferred_element_type=jnp.float32)
    up_terms = jnp.dot(z, up_weight, preferred_element_type=jnp.float32)
    gate, up = lax.psum((gate_terms, up_terms), "dp")
    act, gelu_back = jax.vjp(gelu_tanh, gate)
    hidden = (act * up).astype(jnp.bfloat16)
    branch = lax.psum(jnp.dot(hidden, down_weight, preferred_element_type=jnp.float32), "vocab")
    gained = branch * post_gain
    square_br = lax.psum(jnp.sum(branch * branch, axis=1), "dp")
    rms_br = lax.rsqrt(square_br / D + eps)[:, None]
    stream = xf + gained * rms_br
    square_st = lax.psum(jnp.sum(stream * stream, axis=1), "dp")
    rms_st = lax.rsqrt(square_st / D + eps)[:, None]
    normed_local = (stream * rms_st * final_gain).astype(jnp.bfloat16)
    normed = lax.all_gather(normed_local, "dp", axis=1, tiled=True)
    raw = contract_last(normed, embedding)
    student = softcap_value * jnp.tanh(raw / softcap_value)
    teacher = lax.all_to_all(
        teacher_logits, "vocab", split_axis=1, concat_axis=0, tiled=True
    ).astype(jnp.float32)
    entries = embedding.shape[0]
    columns = lax.axis_index(("dp", "vocab")) * entries + jnp.arange(entries, dtype=jnp.int32)
    onehot = jnp.where(target_ids[:, None] == columns[None, :], 1.0, 0.0).astype(jnp.float32)
    exp_s = jnp.exp(student)
    exp_t = jnp.exp(teacher)
    total_s, total_t, weighted, picked = lax.psum(
        (
            jnp.sum(exp_s, axis=1),
            jnp.sum(exp_t, axis=1),
            jnp.sum(exp_t * (teacher - student), axis=1),
            jnp.sum(onehot * student, axis=1),
        ),
        ("dp", "vocab"),
    )
    log_s = jnp.log(total_s)
    log_t = jnp.log(total_t)
    mask = token_mask(lengths, positions)
    count = jnp.sum(lengths).astype(jnp.float32)
    per_token = weighted / total_t - log_t + log_s + hard_weight * (log_s - picked)
    loss = jnp.sum(mask * per_token) / count
    factor = loss_scale / count * mask[:, None]
    dstudent = factor * (
        (1.0 + hard_weight) * exp_s / total_s[:, None]
        - exp_t / total_t[:, None]
        - hard_weight * onehot
    )
    capped = student / softcap_value
    dlogit = (dstudent * (1.0 - capped * capped)).astype(jnp.bfloat16)
    grad_embedding = contract_first(dlogit, normed).astype(jnp.bfloat16)
    partial_grad = jnp.dot(dlogit, embedding, preferred_element_type=jnp.float32)
    local_grad = lax.psum_scatter(partial_grad, "dp", scatter_dimension=1, tiled=True)
    dnormed = lax.psum(local_grad, "vocab")
    along = dnormed * final_gain
    cube_st = rms_st * rms_st * rms_st
    cube_br = rms_br * rms_br * rms_br
    stream_along = lax.psum(jnp.sum(stream * along, axis=1), "dp")
    dstream = rms_st * along - stream * cube_st * (stream_along[:, None] / D)
    back = dstream * post_gain
    branch_back = lax.psum(jnp.sum(branch * back, axis=1), "dp")
    mean_br = branch_back[:, None] / D
    dbranch = rms_br * back - branch * cube_br * mean_br
    grad_out = dbranch.astype(jnp.bfloat16)
    grad_down = contract_first(hidden, grad_out).astype(jnp.bfloat16)
    dh_terms = contract_last(grad_out, down_weight)
    dh = lax.psum(dh_terms, "dp")
    dgate = gelu_back(dh * up)[0].astype(jnp.bfloat16)
    dup = (dh * act).astype(jnp.bfloat16)
    grad_gate = contract_first(z, dgate).astype(jnp.bfloat16)
    grad_up = contract_first(z, dup).astype(jnp.bfloat16)
    dz = lax.psum(contract_last(dgate, gate_weight) + contract_last(dup, up_weight), "vocab")
    scaled = dz * pre_gain
    input_inner = lax.psum(jnp.sum(xf * scaled, axis=1), "dp")
    cube_in = rms_in * rms_in * rms_in
    dinput = rms_in * scaled - xf * cube_in * (input_inner[:, None] / D)
    grad_hidden = (dstream + dinput).astype(jnp.bfloat16)
    return (loss, grad_hidden, grad_gate, grad_up, grad_down, grad_embedding)


def solution(mesh):
    return jax.shard_map(
        on_device,
        mesh=mesh,
        in_specs=(
            P(None, "dp"),
            P("dp"),
            P("dp", "vocab"),
            P("dp", "vocab"),
            P("vocab", "dp"),
            P("dp"),
            P("dp"),
            P(("dp", "vocab"), None),
            P("vocab", "dp"),
            P(),
            P(),
        ),
        out_specs=(
            P(),
            P(None, "dp"),
            P("dp", "vocab"),
            P("dp", "vocab"),
            P("vocab", "dp"),
            P(("dp", "vocab"), None),
        ),
        check_vma=False,
    )
```

profile of v0, /device:TPU:0, one launch (start us, length us, event | category | flops | bytes accessed | tf_op | source)
XLA Modules:
  0.0 562.4 jit_solution(9600510315278384170)
XLA Ops:
  7.2 1.2 fusion.8
  8.4 15.1 %psum.112 = f32[256]{0:T(256)S(1)} all-reduce(f32[256]{0:T(256)S(1)} %fusion.8), channel_id=1, replica_groups=mesh['dp'=8,'vocab'=4] {'dp'}, use_global_device_ids=true, to_apply=%region_2.0 | all-reduce | flops 256 | bytes 2048 | tf_op jit(solution)/shard_map/psum | solution.py:56
  23.6 5.3 fusion.25
  28.9 3.2 fusion.27
  32.1 115.4 %all-reduce.16.cloned.1.call-done = (f32[256,3584]{1,0:T(8,128)}, f32[256,3584]{1,0:T(8,128)}) async-done(((f32[256,3584]{1,0:T(8,128)}, f32[256,3584]{1,0:T(8,128)}), (f32[256,3584]{1,0:T(8,128)}, f32[256,3584]{1,0:T(8,128)})) %all-reduce.16.cloned.1.call-update) | async-done | bytes 7340048 | tf_op jit(solution)/shard_map/psum | solution.py:61
  147.5 4.4 multiply_convert_fusion.1
  152.0 1.2 copy-done.8
  153.2 1.8 fusion.32
  155.1 37.8 %all-reduce.8.cloned.1.call-done = f32[256,448]{0,1:T(8,128)} async-done(((f32[256,448]{0,1:T(8,128)}), f32[256,448]{0,1:T(8,128)}) %all-reduce.8.cloned.1.call-update) | async-done | bytes 458768 | tf_op jit(solution)/shard_map/psum | solution.py:64
  192.8 1.1 multiply_reduce_fusion.3
  193.9 12.5 %psum.116 = f32[256]{0:T(256)S(1)} all-reduce(f32[256]{0:T(256)S(1)} %multiply_reduce_fusion.3), channel_id=1, replica_groups=mesh['dp'=8,'vocab'=4] {'dp'}, use_global_device_ids=true, to_apply=%region_7.0 | all-reduce | flops 256 | bytes 2048 | tf_op jit(solution)/shard_map/psum | solution.py:66
  206.4 1.2 multiply_reduce_fusion.2
  207.6 11.8 %psum.117 = f32[256]{0:T(256)S(1)} all-reduce(f32[256]{0:T(256)S(1)} %multiply_reduce_fusion.2), channel_id=1, replica_groups=mesh['dp'=8,'vocab'=4] {'dp'}, use_global_device_ids=true, to_apply=%region_9.10 | all-reduce | flops 256 | bytes 2048 | tf_op jit(solution)/shard_map/psum | solution.py:69
  219.4 1.9 multiply_convert_fusion.2
  221.4 1.6 copy.36
  222.9 3.9 all-to-all-start
  226.9 0.6 reduce_sum.132
  228.4 4.8 all-to-all-done
  233.2 1.6 convert_element_type.74
  234.8 1.8 copy.29
  236.6 1.0 exponential_reduce_fusion
  237.9 8.7 %all-gather.2.cloned.1.call-done = bf16[256,3584]{0,1:T(8,128)(2,1)} async-done(((bf16[256,448]{0,1:T(8,128)(2,1)}), bf16[256,3584]{0,1:T(8,128)(2,1)}) %all-gather.2.cloned.1.call-update) | async-done | bytes 1835024 | tf_op jit(solution)/shard_map/all_gather | solution.py:72
  246.6 3.4 multiply_reduce_fusion.4
  250.0 39.3 %all-reduce = (f32[256]{0:T(256)S(1)}, f32[256]{0:T(256)S(1)}, f32[256]{0:T(256)S(1)}, f32[256]{0:T(256)S(1)}) all-reduce(f32[256]{0:T(256)S(1)} %get-tuple-element.8, f32[256]{0:T(256)S(1)} %get-tuple-element.7, f32[256]{0:T(256)S(1)} %reduce_sum.128, f32[256]{0:T(256)S(1)} %get-tuple-element.6), channel_id=1, replica_groups=mesh['dp'=8,'vocab'=4] {'dp','vocab'}, use_global_device_ids=true, to_apply=%region_17.18 | all-reduce | flops 1024 | bytes 8192 | tf_op jit(solution)/shard_map/psum | solution.py:83
  289.9 4.6 fusion.30
  294.6 49.6 %reduce-scatter.2.cloned.1.call-done = f32[256,448]{0,1:T(8,128)} async-done(((f32[256,3584]{0,1:T(8,128)}), f32[256,448]{0,1:T(8,128)}) %reduce-scatter.2.cloned.1.call-update) | async-done | bytes 458768 | tf_op jit(solution)/shard_map/reduce_scatter | solution.py:108
  344.2 39.8 %all-reduce.10.cloned.1.call-done = f32[256,448]{0,1:T(8,128)} async-done(((f32[256,448]{0,1:T(8,128)}), f32[256,448]{0,1:T(8,128)}) %all-reduce.10.cloned.1.call-update) | async-done | bytes 458768 | tf_op jit(solution)/shard_map/psum | solution.py:109
  384.0 1.4 multiply_reduce_fusion.1
  385.3 12.5 %psum.123 = f32[256]{0:T(256)S(1)} all-reduce(f32[256]{0:T(256)S(1)} %multiply_reduce_fusion.1), channel_id=1, replica_groups=mesh['dp'=8,'vocab'=4] {'dp'}, use_global_device_ids=true, to_apply=%region_23.24 | all-reduce | flops 256 | bytes 2048 | tf_op jit(solution)/shard_map/psum | solution.py:113
  397.8 1.4 multiply_reduce_fusion
  399.3 11.8 %psum.124 = f32[256]{0:T(256)S(1)} all-reduce(f32[256]{0:T(256)S(1)} %multiply_reduce_fusion), channel_id=1, replica_groups=mesh['dp'=8,'vocab'=4] {'dp'}, use_global_device_ids=true, to_apply=%region_25.26 | all-reduce | flops 256 | bytes 2048 | tf_op jit(solution)/shard_map/psum | solution.py:116
  411.1 1.4 subtract_convert_fusion
  412.5 0.7 copy-done.10
  413.2 3.1 fusion.33
  417.2 3.8 convolution_convert_fusion.3
  421.0 2.7 convolution_convert_fusion
  423.7 66.3 %all-reduce.12.cloned.1.call-done = f32[256,3584]{1,0:T(8,128)} async-done(((f32[256,3584]{1,0:T(8,128)}), f32[256,3584]{1,0:T(8,128)}) %all-reduce.12.cloned.1.call-update) | async-done | bytes 3670032 | tf_op jit(solution)/shard_map/psum | solution.py:122
  489.9 5.8 %multiply_convert_fusion = (bf16[256,3584]{1,0:T(8,128)(2,1)S(1)}, bf16[256,3584]{1,0:T(8,128)(2,1)S(1)}) fusion(f32[256,3584]{1,0:T(8,128)} %all-reduce.12.cloned.1.call-done, f32[256,3584]{1,0:T(8,128)} %get-tuple-element.14, f32[256,3584]{1,0:T(8,128)} %get-tuple-element.13), kind=kLoop, calls=%fused_computation.13 | loop fusion | flops 22020096 | bytes 14680064 | tf_op jit(solution)/shard_map/convert_element_type | solution.py:124
  495.8 1.0 fusion.34
  496.9 0.6 copy-done.5
  497.6 1.4 copy-done.4
  499.0 1.8 convolution_add_fusion
  500.8 4.4 convolution_convert_fusion.2
  505.2 2.7 convolution_convert_fusion.1
  507.9 30.6 %all-reduce.14.cloned.1.call-done = f32[256,448]{0,1:T(8,128)} async-done(((f32[256,448]{0,1:T(8,128)}), f32[256,448]{0,1:T(8,128)}) %all-reduce.14.cloned.1.call-update) | async-done | bytes 458768 | tf_op jit(solution)/shard_map/psum | solution.py:127
  538.5 1.2 fusion.15
  539.7 12.5 %psum.127 = f32[256]{0:T(256)S(1)} all-reduce(f32[256]{0:T(256)S(1)} %fusion.15), channel_id=1, replica_groups=mesh['dp'=8,'vocab'=4] {'dp'}, use_global_device_ids=true, to_apply=%region_29.30 | all-reduce | flops 256 | bytes 2048 | tf_op jit(solution)/shard_map/psum | solution.py:129
  552.2 2.3 fusion.14
  (57 shorter events, 1.8 us)
Async XLA Ops:
  7.2 146.0 %copy-start = (bf16[3584,448]{0,1:T(8,128)(2,1)S(1)}, bf16[3584,448]{0,1:T(8,128)(2,1)}, u32[]{:S(2)}) copy-start(bf16[3584,448]{0,1:T(8,128)(2,1)} %param.15) | copy-start | bytes 9633796
  7.2 140.4 %all-reduce.16.cloned.1.call-start = ((), (), s32[]{:S(2)}) async-start(), calls=%async_computation.8 | async-start | bytes 14680064 | tf_op jit(solution)/shard_map/psum | solution.py:61
  23.5 5.3 copy-start.1
  23.5 5.3 copy-start.2
  23.5 5.3 copy-start.12
  32.1 160.8 %all-reduce.8.cloned.1.call-start = ((), (), s32[]{:S(2)}) async-start(), calls=%async_computation.2 | async-start | bytes 917504 | tf_op jit(solution)/shard_map/psum | solution.py:64
  152.0 1.2 copy-start.8
  153.2 53.2 %copy-start.13 = (f32[448]{0:T(512)S(1)}, f32[448]{0:T(512)}, u32[]{:S(2)}) copy-start(f32[448]{0:T(512)} %param.16) | copy-start | bytes 5380
  153.2 66.3 %copy-start.14 = (f32[448]{0:T(512)S(1)}, f32[448]{0:T(512)}, u32[]{:S(2)}) copy-start(f32[448]{0:T(512)} %param.17) | copy-start | bytes 5380
  153.2 73.7 %copy-start.16 = (s32[2]{0:T(128)S(1)}, s32[2]{0:T(128)}, u32[]{:S(2)}) copy-start(s32[2]{0:T(128)} %param.21) | copy-start | bytes 28
  155.0 91.6 %copy-start.15 = (s32[256]{0:T(256)S(1)}, s32[256]{0:T(256)}, u32[]{:S(2)}) copy-start(s32[256]{0:T(256)} %param.20) | copy-start | bytes 3076
  155.0 91.6 %all-gather.2.cloned.1.call-start = ((), (), s32[]{:S(2)}) async-start(), calls=%async_computation.3 | async-start | bytes 2064384 | tf_op jit(solution)/shard_map/all_gather | solution.py:72
  222.9 10.2 %all-to-all-start = ((bf16[64,4,256]{2,0,1:T(8,128)(2,1)}), bf16[64,4,256]{2,0,1:T(8,128)(2,1)}, u32[]{:S(2)}, u32[]{:S(2)}) async-start(bf16[64,4,256]{2,0,1:T(8,128)(2,1)} %bitcast.27), calls=%async_computation | async-start | bytes 262144 | tf_op jit(solution)/shard_map/all_to_all | solution.py:75
  226.9 117.3 %reduce-scatter.2.cloned.1.call-start = ((), (), s32[]{:S(2)}) async-start(), calls=%async_computation.4 | async-start | bytes 4128768 | tf_op jit(solution)/shard_map/reduce_scatter | solution.py:108
  294.5 89.5 %all-reduce.10.cloned.1.call-start = ((), (), s32[]{:S(2)}) async-start(), calls=%async_computation.5 | async-start | bytes 917504 | tf_op jit(solution)/shard_map/psum | solution.py:109
  344.2 145.8 %all-reduce.12.cloned.1.call-start = ((), (), s32[]{:S(2)}) async-start(), calls=%async_computation.6 | async-start | bytes 7340032 | tf_op jit(solution)/shard_map/psum | solution.py:122
  412.5 0.7 copy-start.10
  416.3 122.2 %all-reduce.14.cloned.1.call-start = ((), (), s32[]{:S(2)}) async-start(), calls=%async_computation.7 | async-start | bytes 917504 | tf_op jit(solution)/shard_map/psum | solution.py:127
  417.2 3.8 copy-start.9
  417.2 3.8 copy-start.11
  489.9 5.8 %copy-start.3 = (bf16[448,3584]{1,0:T(8,128)(2,1)S(1)}, bf16[448,3584]{1,0:T(8,128)(2,1)}, u32[]{:S(2)}) copy-start(bf16[448,3584]{1,0:T(8,128)(2,1)} %param.13) | copy-start | bytes 9633796
  495.7 1.2 copy-start.7
  495.7 1.9 copy-start.5
  495.7 3.2 copy-start.4
  500.8 4.4 copy-start.6
Sparse Core Ops, SparseCore 0:
  32.2 115.3 all-reduce.15
  155.1 37.6 all-reduce.7
  221.5 25.0 all-gather.1
  294.6 49.4 reduce-scatter.1
  346.5 37.4 all-reduce.9
  416.4 73.4 all-reduce.11
  500.9 37.5 all-reduce.13
where the time goes:
time: 563 us; the launch traced here: 562 us
  waiting for transfers between devices  353 us (63%)
  blocking collectives  115 us (20%)
  matrix products  37.7 us (7%)
  other arithmetic  27.2 us (5%)
  between operations  16.8 us (3%)
  local copies, waits for them, and re-layouts  7.77 us (1%)
    psum x1, waiting for transfers between devices, on_device(): gate, up = lax.psum((gate_terms, up_terms), 'dp')  115 us
    psum x1, waiting for transfers between devices, on_device(): dh = lax.psum(dh_terms, 'dp')  66.3 us
    reduce_scatter x1, waiting for transfers between devices, on_device(): lax.psum_scatter(partial_grad, 'dp', scatter_dimension=1, tiled=True)  49.6 us
    psum x1, waiting for transfers between devices, on_device(): dnormed = lax.psum(local_grad, 'vocab')  39.8 us
    psum x1, blocking collectives, on_device(): lax.psum((jnp.sum(exp_s, axis=1), jnp.sum(exp_t, axis=1), jnp.sum(exp_t *...  39.3 us
    psum x1, waiting for transfers between devices, on_device(): lax.psum(jnp.dot(hidden, down_weight, preferred_element_type=jnp.float32)...  37.8 us
    psum x1, waiting for transfers between devices, on_device(): lax.psum(contract_last(dgate, gate_weight) + contract_last(dup, up_weight...  30.6 us
    psum x1, blocking collectives, on_device(): square_in = lax.psum(jnp.sum(xf * xf, axis=1), 'dp')  15.1 us
  transfers between devices with their start and end apart: 8, of which 8 were waited for; matrix products, arithmetic and copies ran while one was open for 4% of the time, Pallas kernels for 0%

commit v1 on v0

--- a/solution.py
+++ b/solution.py
@@ -1,6 +1,9 @@
+import functools
 import jax
 import jax.numpy as jnp
 from jax import lax
+from jax.experimental import pallas as pl
+from jax.experimental.pallas import tpu as pltpu
 from jax.sharding import PartitionSpec as P
 
 D = 3584
@@ -38,7 +41,7 @@
     )
 
 
-def on_device(
+def on_device_plain(
     hidden_in,
     pre_gain,
     gate_weight,
@@ -133,9 +136,321 @@
     return (loss, grad_hidden, grad_gate, grad_up, grad_down, grad_embedding)
 
 
+MESH_ID = pl.DeviceIdType.MESH
+CUBE = 0.044715
+ROOT = 0.7978845608028654
+TILE = 512
+
+
+def vmem():
+    return pl.BlockSpec(memory_space=pltpu.VMEM)
+
+
+def send(src, dst, sems, slot, peer):
+    copy = pltpu.make_async_remote_copy(
+        src_ref=src,
+        dst_ref=dst,
+        send_sem=sems.at[0, slot],
+        recv_sem=sems.at[1, slot],
+        device_id=peer,
+        device_id_type=MESH_ID,
+    )
+    copy.start()
+    return copy
+
+
+def greet(peers):
+    barrier = pltpu.get_barrier_semaphore()
+    for peer in peers:
+        pl.semaphore_signal(barrier, inc=1, device_id=peer, device_id_type=MESH_ID)
+    pl.semaphore_wait(barrier, len(peers))
+
+
+def places(chips):
+    dp = lax.axis_index("dp")
+    z = lax.axis_index("vocab")
+    chip, core = dp // 2, dp % 2
+    sibling = (chip * 2 + 1 - core, z)
+    others = [(((chip + k) % chips) * 2 + core, z) for k in range(1, chips)]
+    return chip, core, sibling, others
+
+
+def scatter_sum(chips, part, got_pair, out_chip, got_chip, sems, base):
+    chip, core, sibling, others = places(chips)
+    order = list(range(1, chips)) + [0]
+    pair = {}
+    for k in order:
+        there = (chip + k) % chips
+        pair[k] = send(part.at[there, 1 - core], got_pair.at[there], sems, base + k, sibling)
+    far = {}
+    width = part.shape[-1]
+    step = min(TILE, width)
+    for k in order:
+        there = (chip + k) % chips
+        pair[k].wait_recv()
+        if k:
+            for at in range(0, width, step):
+                cols = pl.ds(at, step)
+                total = part[there, core, :, cols].astype(jnp.float32) + got_pair[
+                    there, :, cols
+                ].astype(jnp.float32)
+                out_chip[k - 1, :, cols] = total.astype(out_chip.dtype)
+            far[k] = send(
+                out_chip.at[k - 1], got_chip.at[k - 1], sems, base + chips + k, others[k - 1]
+            )
+    for k in range(1, chips):
+        far[k].wait_recv()
+
+    def take(rows, cols):
+        total = part[chip, core, rows, cols].astype(jnp.float32) + got_pair[
+            chip, rows, cols
+        ].astype(jnp.float32)
+        for k in range(1, chips):
+            total += got_chip[k - 1, rows, cols].astype(jnp.float32)
+        return total
+
+    return take, list(pair.values()) + list(far.values())
+
+
+def gather_blocks(chips, out, sems, base):
+    chip, core, sibling, others = places(chips)
+    mine = out.at[chip, core]
+    sent = [
+        send(mine, mine, sems, base + k, others[k - 1]) for k in range(1, chips)
+    ]
+    near = send(mine, mine, sems, base, sibling)
+    passed = []
+    for k in range(1, chips):
+        sent[k - 1].wait_recv()
+        origin = (chip + chips - k) % chips
+        block = out.at[origin, core]
+        passed.append(send(block, block, sems, base + chips + k, sibling))
+    near.wait_recv()
+    for copy in passed:
+        copy.wait_recv()
+    return sent + [near] + passed
+
+
+def finish(copies):
+    for copy in copies:
+        copy.wait_send()
+
+
+def ffn_kernel(
+    chips, rows, x_ref, square_ref, gate_ref, up_ref,
+    h_ref, act_ref, slope_ref,
+    part, got_pair, out_chip, got_chip, sq, sq_pair, sq_out, sq_chip, sems,
+):
+    chip, core, sibling, others = places(chips)
+    greet([sibling] + others)
+    ff = gate_ref.shape[1]
+    sq[...] = square_ref[...].reshape(sq.shape)
+    for at in range(0, ff, TILE):
+        cols = pl.ds(at, TILE)
+        for which, weight in ((0, gate_ref), (1, up_ref)):
+            terms = jnp.dot(x_ref[...], weight[:, cols], preferred_element_type=jnp.float32)
+            part[:, :, pl.ds(which * rows, rows), cols] = terms.astype(jnp.bfloat16).reshape(
+                chips, 2, rows, TILE
+            )
+    take_sq, sent_sq = scatter_sum(chips, sq, sq_pair, sq_out, sq_chip, sems, 0)
+    take, sent = scatter_sum(chips, part, got_pair, out_chip, got_chip, sems, 2 * chips)
+    rms = lax.rsqrt(take_sq(pl.ds(0, rows), pl.ds(0, 128))[:, :1] / D + eps)
+    for at in range(0, ff, TILE):
+        cols = pl.ds(at, TILE)
+        gate = take(pl.ds(0, rows), cols) * rms
+        up = take(pl.ds(rows, rows), cols) * rms
+        square = gate * gate
+        bend = jnp.tanh(ROOT * (gate + CUBE * gate * square))
+        half = 0.5 * (1.0 + bend)
+        act = gate * half
+        slope = half + 0.5 * gate * (1.0 - bend * bend) * (ROOT * (1.0 + 3.0 * CUBE * square))
+        h_ref[chip, core, :, cols] = (act * up).astype(jnp.bfloat16)
+        act_ref[:, cols] = act * rms
+        slope_ref[:, cols] = up * slope * rms
+    finish(sent_sq + sent + gather_blocks(chips, h_ref, sems, 4 * chips))
+
+
+def ffn_forward(chips, x_gained, squares, gate_weight, up_weight):
+    tokens = x_gained.shape[0]
+    ff = gate_weight.shape[1]
+    rows = tokens // (2 * chips)
+    b16, f32 = jnp.bfloat16, jnp.float32
+    return pl.pallas_call(
+        functools.partial(ffn_kernel, chips, rows),
+        out_shape=(
+            jax.ShapeDtypeStruct((chips, 2, rows, ff), b16),
+            jax.ShapeDtypeStruct((rows, ff), f32),
+            jax.ShapeDtypeStruct((rows, ff), f32),
+        ),
+        in_specs=[vmem()] * 4,
+        out_specs=(vmem(),) * 3,
+        scratch_shapes=[
+            pltpu.VMEM((chips, 2, 2 * rows, ff), b16),
+            pltpu.VMEM((chips, 2 * rows, ff), b16),
+            pltpu.VMEM((chips - 1, 2 * rows, ff), b16),
+            pltpu.VMEM((chips - 1, 2 * rows, ff), b16),
+            pltpu.VMEM((chips, 2, rows, 128), f32),
+            pltpu.VMEM((chips, rows, 128), f32),
+            pltpu.VMEM((chips - 1, rows, 128), f32),
+            pltpu.VMEM((chips - 1, rows, 128), f32),
+            pltpu.SemaphoreType.DMA((2, 6 * chips)),
+        ],
+        compiler_params=pltpu.CompilerParams(
+            collective_id=1, has_side_effects=True, vmem_limit_bytes=48 * 2**20
+        ),
+    )(x_gained, squares, gate_weight, up_weight)
+
+
+def hidden_kernel(
+    chips, rows, dy_ref, down_ref, act_ref, slope_ref,
+    pair_ref, part, got_pair, out_chip, got_chip, sems,
+):
+    chip, core, sibling, others = places(chips)
+    greet([sibling] + others)
+    ff = down_ref.shape[0]
+    for at in range(0, ff, TILE):
+        cols = pl.ds(at, TILE)
+        terms = contract_last(dy_ref[...], down_ref[cols, :])
+        part[:, :, :, cols] = terms.astype(jnp.bfloat16).reshape(chips, 2, rows, TILE)
+    take, sent = scatter_sum(chips, part, got_pair, out_chip, got_chip, sems, 0)
+    for at in range(0, ff, TILE):
+        cols = pl.ds(at, TILE)
+        dh = take(pl.ds(0, rows), cols)
+        pair_ref[chip, core, 0, :, cols] = (dh * slope_ref[:, cols]).astype(jnp.bfloat16)
+        pair_ref[chip, core, 1, :, cols] = (dh * act_ref[:, cols]).astype(jnp.bfloat16)
+    finish(sent + gather_blocks(chips, pair_ref, sems, 2 * chips))
+
+
+def hidden_backward(chips, dy, down_weight, act, slope):
+    tokens = dy.shape[0]
+    ff = down_weight.shape[0]
+    rows = tokens // (2 * chips)
+    b16 = jnp.bfloat16
+    return pl.pallas_call(
+        functools.partial(hidden_kernel, chips, rows),
+        out_shape=jax.ShapeDtypeStruct((chips, 2, 2, rows, ff), b16),
+        in_specs=[vmem()] * 4,
+        out_specs=vmem(),
+        scratch_shapes=[
+            pltpu.VMEM((chips, 2, rows, ff), b16),
+            pltpu.VMEM((chips, rows, ff), b16),
+            pltpu.VMEM((chips - 1, rows, ff), b16),
+            pltpu.VMEM((chips - 1, rows, ff), b16),
+            pltpu.SemaphoreType.DMA((2, 4 * chips)),
+        ],
+        compiler_params=pltpu.CompilerParams(
+            collective_id=2, has_side_effects=True, vmem_limit_bytes=48 * 2**20
+        ),
+    )(dy, down_weight, act, slope)
+
+
+def on_device(
+    chips,
+    hidden_in,
+    pre_gain,
+    gate_weight,
+    up_weight,
+    down_weight,
+    post_gain,
+    final_gain,
+    embedding,
+    teacher_logits,
+    target_ids,
+    lengths,
+):
+    positions = hidden_in.shape[0]
+    xf = hidden_in.astype(jnp.float32)
+    x_gained = (xf * pre_gain).astype(jnp.bfloat16)
+    square_local = jnp.sum(xf * xf, axis=1)
+    h_blocks, act, slope = ffn_forward(
+        chips,
+        x_gained,
+        jnp.broadcast_to(square_local[:, None], (positions, 128)),
+        gate_weight,
+        up_weight,
+    )
+    hidden = h_blocks.reshape(positions, -1)
+    branch = lax.psum(jnp.dot(hidden, down_weight, preferred_element_type=jnp.float32), "vocab")
+    gained = branch * post_gain
+    square_br = lax.psum(jnp.sum(branch * branch, axis=1), "dp")
+    rms_br = lax.rsqrt(square_br / D + eps)[:, None]
+    stream = xf + gained * rms_br
+    square_st = lax.psum(jnp.sum(stream * stream, axis=1), "dp")
+    rms_st = lax.rsqrt(square_st / D + eps)[:, None]
+    normed_local = (stream * rms_st * final_gain).astype(jnp.bfloat16)
+    normed = lax.all_gather(normed_local, "dp", axis=1, tiled=True)
+    raw = contract_last(normed, embedding)
+    student = softcap_value * jnp.tanh(raw / softcap_value)
+    teacher = lax.all_to_all(
+        teacher_logits, "vocab", split_axis=1, concat_axis=0, tiled=True
+    ).astype(jnp.float32)
+    entries = embedding.shape[0]
+    columns = lax.axis_index(("dp", "vocab")) * entries + jnp.arange(entries, dtype=jnp.int32)
+    onehot = jnp.where(target_ids[:, None] == columns[None, :], 1.0, 0.0).astype(jnp.float32)
+    exp_s = jnp.exp(student)
+    exp_t = jnp.exp(teacher)
+    total_s, total_t, weighted, picked = lax.psum(
+        (
+            jnp.sum(exp_s, axis=1),
+            jnp.sum(exp_t, axis=1),
+            jnp.sum(exp_t * (teacher - student), axis=1),
+            jnp.sum(onehot * student, axis=1),
+        ),
+        ("dp", "vocab"),
+    )
+    log_s = jnp.log(total_s)
+    log_t = jnp.log(total_t)
+    mask = token_mask(lengths, positions)
+    count = jnp.sum(lengths).astype(jnp.float32)
+    per_token = weighted / total_t - log_t + log_s + hard_weight * (log_s - picked)
+    loss = jnp.sum(mask * per_token) / count
+    factor = loss_scale / count * mask[:, None]
+    dstudent = factor * (
+        (1.0 + hard_weight) * exp_s / total_s[:, None]
+        - exp_t / total_t[:, None]
+        - hard_weight * onehot
+    )
+    capped = student / softcap_value
+    dlogit = (dstudent * (1.0 - capped * capped)).astype(jnp.bfloat16)
+    grad_embedding = contract_first(dlogit, normed).astype(jnp.bfloat16)
+    partial_grad = jnp.dot(dlogit, embedding, preferred_element_type=jnp.float32)
+    local_grad = lax.psum_scatter(partial_grad, "dp", scatter_dimension=1, tiled=True)
+    dnormed = lax.psum(local_grad, "vocab")
+    along = dnormed * final_gain
+    cube_st = rms_st * rms_st * rms_st
+    cube_br = rms_br * rms_br * rms_br
+    stream_along = lax.psum(jnp.sum(stream * along, axis=1), "dp")
+    dstream = rms_st * along - stream * cube_st * (stream_along[:, None] / D)
+    back = dstream * post_gain
+    branch_back = lax.psum(jnp.sum(branch * back, axis=1), "dp")
+    mean_br = branch_back[:, None] / D
+    dbranch = rms_br * back - branch * cube_br * mean_br
+    grad_out = dbranch.astype(jnp.bfloat16)
+    pairs = hidden_backward(chips, grad_out, down_weight, act, slope)
+    dgate = pairs[:, :, 0].reshape(positions, -1)
+    dup = pairs[:, :, 1].reshape(positions, -1)
+    grad_down = contract_first(hidden, grad_out).astype(jnp.bfloat16)
+    grad_gate = contract_first(x_gained, dgate).astype(jnp.bfloat16)
+    grad_up = contract_first(x_gained, dup).astype(jnp.bfloat16)
+    dz = lax.psum(contract_last(dgate, gate_weight) + contract_last(dup, up_weight), "vocab")
+    scaled = dz * pre_gain
+    input_inner, square_in = lax.psum((jnp.sum(xf * scaled, axis=1), square_local), "dp")
+    mean_in = 1.0 / (square_in / D + eps) * (input_inner / D)
+    grad_hidden = (dstream + scaled - xf * mean_in[:, None]).astype(jnp.bfloat16)
+    return (loss, grad_hidden, grad_gate, grad_up, grad_down, grad_embedding)
+
+
+def pick_plan(mesh):
+    chips = mesh.shape["dp"] // 2
+    tokens = LENGTH * 2
+    if mesh.shape["dp"] % 2 == 0 and chips > 1 and tokens % (32 * chips) == 0:
+        return functools.partial(on_device, chips)
+    return on_device_plain
+
+
 def solution(mesh):
     return jax.shard_map(
-        on_device,
+        pick_plan(mesh),
         mesh=mesh,
         in_specs=(
             P(None, "dp"),

time: 563 us -> 440 us (0.78)
  waiting for transfers between devices: 353 us -> 162 us
  Pallas kernels: 0 us -> 92.2 us
  matrix products: 37.7 us -> 24.1 us
  blocking collectives: 115 us -> 103 us
  local copies, waits for them, and re-layouts: 7.77 us -> 19.6 us
  other arithmetic: 27.2 us -> 18.2 us
    psum x2 -> x0, waiting for transfers between devices: 182 us -> none  [the longest x1 115 us: on_device(): gate, up = lax.psum((gate_terms, up_terms), 'dp')]
    pallas_call x0 -> x2, Pallas kernels: none -> 92.2 us  [the longest x1 50.6 us: ffn_forward(): pl.pallas_call(functools.partial(ffn_kernel, chips, rows), out_shape=(jax...]
    reduce_scatter x1 -> x0, waiting for transfers between devices: 49.6 us -> none  [on_device(): lax.psum_scatter(partial_grad, 'dp', scatter_dimension=1, tiled=True)]
    unnamed x7 -> x6, waiting for transfers between devices: 0.11 us -> 49.7 us
    psum x2 -> x1, blocking collectives: 27.6 us -> 12.9 us  [on_device(): lax.psum((jnp.sum(xf * scaled, axis=1), square_local), 'dp')]
    dot_general x3 -> x0, matrix products: 13 us -> none  [the longest x1 5.32 us: on_device(): up_terms = jnp.dot(z, up_weight, preferred_element_type=jnp.float32)]
    convert_element_type x3 -> x1, other arithmetic: 12.5 us -> 1.51 us  [on_device(): (dstream + scaled - xf * mean_in[:, None]).astype(jnp.bfloat16)]
    psum x1, waiting for transfers between devices: 39.8 us -> 28.9 us  [on_device(): dnormed = lax.psum(local_grad, 'vocab')]
  transfers between devices with their start and end apart: 8 -> 6, of which waited for: 8 -> 6; matrix products, arithmetic and copies ran while one was open for 4% -> 5% of each run, Pallas kernels for 0% -> 0%
where the time goes in v1:
time: 440 us; the launch traced here: 439 us
  waiting for transfers between devices  162 us (37%)
  blocking collectives  103 us (23%)
  Pallas kernels  92.2 us (21%)
  matrix products  24.1 us (5%)
  local copies, waits for them, and re-layouts  19.6 us (4%)
  other arithmetic  18.2 us (4%)
  between operations  16.5 us (4%)
    pallas_call x1, Pallas kernels, ffn_forward(): pl.pallas_call(functools.partial(ffn_kernel, chips, rows), out_shape=(jax...  50.6 us
    unnamed x6, waiting for transfers between devices  49.7 us
    pallas_call x1, Pallas kernels, hidden_backward(): pl.pallas_call(functools.partial(hidden_kernel, chips, rows), out_shape=j...  41.7 us
    psum x1, blocking collectives, on_device(): lax.psum((jnp.sum(exp_s, axis=1), jnp.sum(exp_t, axis=1), jnp.sum(exp_t *...  39.3 us
    psum x1, waiting for transfers between devices, on_device(): lax.psum(jnp.dot(hidden, down_weight, preferred_element_type=jnp.float32)...  38.9 us
    psum x1, waiting for transfers between devices, on_device(): lax.psum(contract_last(dgate, gate_weight) + contract_last(dup, up_weight...  29.6 us
    psum x1, waiting for transfers between devices, on_device(): dnormed = lax.psum(local_grad, 'vocab')  28.9 us
    unnamed x55, local copies, waits for them, and re-layouts  14.6 us
  transfers between devices with their start and end apart: 6, of which 6 were waited for; matrix products, arithmetic and copies ran while one was open for 5% of the time, Pallas kernels for 0%

profile of v1, /device:TPU:0, one launch (start us, length us, event | category | flops | bytes accessed | tf_op | source)
XLA Modules:
  0.0 439.0 jit_solution(4646948713115720808)
XLA Ops:
  7.2 1.2 copy.72
  8.4 0.9 fusion.2
  9.9 50.6 %shard_map.154 = (bf16[4,2,32,3584]{3,2,1,0:T(8,128)(2,1)S(1)}, f32[32,3584]{1,0:T(8,128)S(1)}, f32[32,3584]{1,0:T(8,128)S(1)}) custom-call(bf16[256,448]{1,0:T(8,128)(2,1)S(1)} %get-tuple-element.60.x_ref, f32[256,128]{1,0:T(8,128)S(1)} %broadcast_in_dim.34.square_ref, bf16[448,3584]{1,0:T(8,128)(2,1)} %gate_ref.1, bf16[448,3584]{1,0:T(8,128)(2,1)} %up_ref.1), custom_call_target="tpu_custom_call" | custom-call | tf_op jit(solution)/shard_map/pallas_call | solution.py:278
  60.5 1.2 copy-done.1
  61.8 1.9 fusion.16
  63.8 38.9 %all-reduce.6.cloned.1.call-done = f32[256,448]{1,0:T(8,128)} async-done(((f32[256,448]{1,0:T(8,128)}), f32[256,448]{1,0:T(8,128)}) %all-reduce.6.cloned.1.call-update) | async-done | bytes 458768 | tf_op jit(solution)/shard_map/psum | solution.py:373
  102.7 1.2 multiply_reduce_fusion.3
  103.9 12.9 %psum.92 = f32[256]{0:T(256)S(1)} all-reduce(f32[256]{0:T(256)S(1)} %multiply_reduce_fusion.3), channel_id=1, replica_groups=mesh['dp'=8,'vocab'=4] {'dp'}, use_global_device_ids=true, to_apply=%region_4.0 | all-reduce | flops 256 | bytes 2048 | tf_op jit(solution)/shard_map/psum | solution.py:375
  117.3 1.3 multiply_reduce_fusion.2
  118.6 11.8 %psum.93 = f32[256]{0:T(256)S(1)} all-reduce(f32[256]{0:T(256)S(1)} %multiply_reduce_fusion.2), channel_id=1, replica_groups=mesh['dp'=8,'vocab'=4] {'dp'}, use_global_device_ids=true, to_apply=%region_6.7 | all-reduce | flops 256 | bytes 2048 | tf_op jit(solution)/shard_map/psum | solution.py:378
  131.0 1.2 multiply_convert_fusion
  132.2 0.8 copy.74
  133.0 1.6 copy.89
  134.6 3.3 all-to-all-start
  138.0 1.3 reduce_sum.132
  140.0 0.7 fusion.11
  140.8 3.4 all-to-all-done
  144.1 0.7 convert_element_type.62
  144.9 1.1 copy.71
  146.3 11.7 %all-gather.2.cloned.1.call-done = bf16[256,3584]{0,1:T(8,128)(2,1)} async-done(((bf16[256,448]{0,1:T(8,128)(2,1)}), bf16[256,3584]{0,1:T(8,128)(2,1)}) %all-gather.2.cloned.1.call-update) | async-done | bytes 1835024 | tf_op jit(solution)/shard_map/all_gather | solution.py:381
  158.0 2.9 multiply_reduce_fusion.4
  160.9 39.3 %all-reduce = (f32[256]{0:T(256)S(1)}, f32[256]{0:T(256)S(1)}, f32[256]{0:T(256)S(1)}, f32[256]{0:T(256)S(1)}) all-reduce(f32[256]{0:T(256)S(1)} %get-tuple-element.50, f32[256]{0:T(256)S(1)} %get-tuple-element.49, f32[256]{0:T(256)S(1)} %reduce_sum.128, f32[256]{0:T(256)S(1)} %get-tuple-element.48), channel_id=1, replica_groups=mesh['dp'=8,'vocab'=4] {'dp','vocab'}, use_global_device_ids=true, to_apply=%region_14.15 | all-reduce | flops 1024 | bytes 8192 | tf_op jit(solution)/shard_map/psum | solution.py:392
  200.2 0.6 broadcast_multiply_fusion
  200.8 3.7 convolution_bitcast_fusion
  204.6 49.6 %reduce-scatter.4.cloned.1.call-done = f32[448,256]{1,0:T(8,128)} async-done(((f32[3584,256]{1,0:T(8,128)}), f32[448,256]{1,0:T(8,128)}) %reduce-scatter.4.cloned.1.call-update) | async-done | bytes 458768
  254.2 2.0 copy.85
  256.3 5.7 %copy.79.down_ref = bf16[3584,448]{1,0:T(8,128)(2,1)} copy(bf16[3584,448]{0,1:T(8,128)(2,1)} %param.15) | data formatting | bytes 6422528 | tf_op args[4]
  262.7 3.8 convolution_convert_fusion.3
  266.5 28.9 %all-reduce.8.cloned.1.call-done = f32[256,448]{1,0:T(8,128)} async-done(((f32[256,448]{1,0:T(8,128)}), f32[256,448]{1,0:T(8,128)}) %all-reduce.8.cloned.1.call-update) | async-done | bytes 458768 | tf_op jit(solution)/shard_map/psum | solution.py:418
  295.4 1.9 multiply_reduce_fusion.1
  297.4 13.6 %psum.99 = f32[256]{0:T(256)} all-reduce(f32[256]{0:T(256)} %multiply_reduce_fusion.1), channel_id=1, replica_groups=mesh['dp'=8,'vocab'=4] {'dp'}, use_global_device_ids=true, to_apply=%region_20.21 | all-reduce | flops 256 | bytes 2048 | tf_op jit(solution)/shard_map/psum | solution.py:422
  310.9 0.7 broadcast_multiply_fusion.2
  312.2 2.1 multiply_reduce_fusion
  314.3 12.1 %psum.100 = f32[256]{0:T(256)S(1)} all-reduce(f32[256]{0:T(256)} %multiply_reduce_fusion), channel_id=1, replica_groups=mesh['dp'=8,'vocab'=4] {'dp'}, use_global_device_ids=true, to_apply=%region_22.23 | all-reduce | flops 256 | bytes 2048 | tf_op jit(solution)/shard_map/psum | solution.py:425
  326.4 1.6 subtract_convert_fusion.dy_ref
  328.0 41.7 %shard_map.155 = bf16[4,2,2,32,3584]{4,3,2,1,0:T(8,128)(2,1)S(1)} custom-call(bf16[256,448]{1,0:T(8,128)(2,1)S(1)} %subtract_convert_fusion.dy_ref, bf16[3584,448]{1,0:T(8,128)(2,1)} %copy.79.down_ref, f32[32,3584]{1,0:T(8,128)S(1)} %get-tuple-element.10.act_ref, f32[32,3584]{1,0:T(8,128)S(1)} %get-tuple-element.11.slope_ref), custom_call_target="tpu_custom_call" | custom-call | tf_op jit(solution)/shard_map/pallas_call | solution.py:329
  370.0 2.2 copy-done.9
  372.2 1.0 fusion.17
  373.3 2.7 convolution_convert_fusion.2
  376.0 1.0 convolution_add_fusion
  377.0 1.0 copy.80
  378.1 4.3 convolution_convert_fusion.1
  382.5 2.7 convolution_convert_fusion
  385.2 29.6 %all-reduce.10.cloned.1.call-done = f32[256,448]{1,0:T(8,128)} async-done(((f32[256,448]{1,0:T(8,128)}), f32[256,448]{1,0:T(8,128)}) %all-reduce.10.cloned.1.call-update) | async-done | bytes 458768 | tf_op jit(solution)/shard_map/psum | solution.py:435
  414.8 1.2 fusion.3
  416.0 12.9 %all-reduce.1 = (f32[256]{0:T(256)S(1)}, f32[256]{0:T(256)S(1)}) all-reduce(f32[256]{0:T(256)S(1)} %fusion.3, f32[256]{0:T(256)S(1)} %copy-done.22), channel_id=1, replica_groups=mesh['dp'=8,'vocab'=4] {'dp'}, use_global_device_ids=true, to_apply=%region_26.27 | all-reduce | flops 512 | bytes 4096 | tf_op jit(solution)/shard_map/psum | solution.py:437
  429.0 1.5 fusion.5
  430.5 0.8 copy.81
  (70 shorter events, 3.4 us)
Async XLA Ops:
  7.2 150.8 %copy-start = (bf16[256,3584]{1,0:T(8,128)(2,1)S(1)}, bf16[256,3584]{1,0:T(8,128)(2,1)}, u32[]{:S(2)}) copy-start(bf16[256,3584]{1,0:T(8,128)(2,1)} %param.18) | copy-start | bytes 5505028
  7.2 95.5 %all-reduce.6.cloned.1.call-start = ((), (), s32[]{:S(2)}) async-start(), calls=%async_computation.2 | async-start | bytes 1048576 | tf_op jit(solution)/shard_map/psum | solution.py:373
  8.4 122.5 %copy-start.5 = (bf16[256,448]{1,0:T(8,128)(2,1)}, bf16[256,448]{1,0:T(8,128)(2,1)S(1)}, u32[]{:S(2)}) copy-start(bf16[256,448]{1,0:T(8,128)(2,1)S(1)} %copy.72) | copy-start | bytes 688132
  9.3 0.5 copy-start.21
  9.9 51.8 %copy-start.8 = (bf16[3584,448]{0,1:T(8,128)(2,1)S(1)}, bf16[3584,448]{0,1:T(8,128)(2,1)}, u32[]{:S(2)}) copy-start(bf16[3584,448]{0,1:T(8,128)(2,1)} %param.15) | copy-start | bytes 9633796
  60.5 1.3 copy-start.1
  61.8 55.5 %copy-start.12 = (f32[448]{0:T(512)S(1)}, f32[448]{0:T(512)}, u32[]{:S(2)}) copy-start(f32[448]{0:T(512)} %param.16) | copy-start | bytes 5380
  63.7 67.3 %copy-start.13 = (f32[448]{0:T(512)S(1)}, f32[448]{0:T(512)}, u32[]{:S(2)}) copy-start(f32[448]{0:T(512)} %param.17) | copy-start | bytes 5380
  63.7 94.3 %all-gather.2.cloned.1.call-start = ((), (), s32[]{:S(2)}) async-start(), calls=%async_computation.3 | async-start | bytes 2064384 | tf_op jit(solution)/shard_map/all_gather | solution.py:381
  134.6 9.5 %all-to-all-start = ((bf16[64,4,256]{2,0,1:T(8,128)(2,1)}), bf16[64,4,256]{2,0,1:T(8,128)(2,1)S(1)}, u32[]{:S(2)}, u32[]{:S(2)}) async-start(bf16[64,4,256]{2,0,1:T(8,128)(2,1)} %bitcast.29), calls=%async_computation | async-start | bytes 262144 | tf_op jit(solution)/shard_map/all_to_all | solution.py:384
  138.0 116.2 %reduce-scatter.4.cloned.1.call-start = ((), (), s32[]{:S(2)}) async-start(), calls=%async_computation.6 | async-start | bytes 4128768
  140.0 60.8 %copy-start.24 = (s32[256]{0:T(256)}, s32[256]{0:T(256)S(1)}, u32[]{:S(2)}) copy-start(s32[256]{0:T(256)S(1)} %iota_add_fusion) | copy-start | bytes 3076
  145.9 54.9 %copy-start.11 = (f32[256,256]{0,1:T(8,128)}, f32[256,256]{0,1:T(8,128)S(1)}, u32[]{:S(2)}) copy-start(f32[256,256]{0,1:T(8,128)S(1)} %copy.71) | copy-start | bytes 786436
  146.3 54.5 %copy-start.23 = (s32[256]{0:T(256)S(1)}, s32[256]{0:T(256)}, u32[]{:S(2)}) copy-start(s32[256]{0:T(256)} %param.20) | copy-start | bytes 3076
  200.2 4.4 copy-start.18
  200.2 4.4 copy-start.19
  200.8 3.8 copy-start.20
  204.6 90.8 %all-reduce.8.cloned.1.call-start = ((), (), s32[]{:S(2)}) async-start(), calls=%async_computation.4 | async-start | bytes 1048576 | tf_op jit(solution)/shard_map/psum | solution.py:418
  256.2 158.6 %all-reduce.10.cloned.1.call-start = ((), (), s32[]{:S(2)}) async-start(), calls=%async_computation.5 | async-start | bytes 1048576 | tf_op jit(solution)/shard_map/psum | solution.py:435
  262.7 32.7 %copy-start.3 = (f32[256,448]{1,0:T(8,128)S(1)}, f32[256,448]{1,0:T(8,128)}, u32[]{:S(2)}) copy-start(f32[256,448]{1,0:T(8,128)} %all-reduce.6.cloned.1.call-done) | copy-start | bytes 1376260
  311.6 0.6 copy-start.16
  369.7 2.6 copy-start.9
  370.0 6.0 %copy-start.7 = (bf16[4,2,1,32,3584]{4,3,2,1,0:T(8,128)(2,1)}, bf16[4,2,1,32,3584]{4,3,2,1,0:T(8,128)(2,1)S(1)}, u32[]{:S(2)}) copy-start(bf16[4,2,1,32,3584]{4,3,2,1,0:T(8,128)(2,1)S(1)} %get-tuple-element.57) | copy-start | bytes 5505028
  373.3 2.7 copy-start.10
  378.1 4.4 copy-start.2
  382.4 32.4 %copy-start.6 = (bf16[256,448]{1,0:T(8,128)(2,1)S(1)}, bf16[256,448]{1,0:T(8,128)(2,1)}, u32[]{:S(2)}) copy-start(bf16[256,448]{1,0:T(8,128)(2,1)} %copy-done.5) | copy-start | bytes 688132
  382.4 32.4 %copy-start.14 = (f32[448]{0:T(512)S(1)}, f32[448]{0:T(512)}, u32[]{:S(2)}) copy-start(f32[448]{0:T(512)} %param.12) | copy-start | bytes 5380
  382.4 33.6 %copy-start.22 = (f32[256]{0:T(256)S(1)}, f32[256]{0:T(256)}, u32[]{:S(2)}) copy-start(f32[256]{0:T(256)} %copy-done.21) | copy-start | bytes 3076
  382.4 46.5 %copy-start.4 = (f32[256,448]{1,0:T(8,128)S(1)}, f32[256,448]{1,0:T(8,128)}, u32[]{:S(2)}) copy-start(f32[256,448]{1,0:T(8,128)} %all-reduce.6.cloned.1.call-done) | copy-start | bytes 1376260
  382.4 46.5 %copy-start.15 = (f32[256]{0:T(256)S(1)}, f32[256]{0:T(256)}, u32[]{:S(2)}) copy-start(f32[256]{0:T(256)} %get-tuple-element.63) | copy-start | bytes 3076
  382.5 46.5 %copy-start.17 = (f32[256]{0:T(256)S(1)}, f32[256]{0:T(256)}, u32[]{:S(2)}) copy-start(f32[256]{0:T(256)} %copy-done.16) | copy-start | bytes 3076
Sparse Core Ops, SparseCore 0:
  63.8 38.8 all-reduce.5
  133.2 24.7 all-gather.1
  204.7 49.4 reduce-scatter.3
  257.1 38.2 all-reduce.7
  378.2 36.5 all-reduce.9

commit v2 on v1

--- a/solution.py
+++ b/solution.py
@@ -344,8 +344,383 @@
     )(dy, down_weight, act, slope)
 
 
+def spots(chips, depth):
+    dp = lax.axis_index("dp")
+    z = lax.axis_index("vocab")
+    chip, core = dp // 2, dp % 2
+    group = [(lax.rem(dp + k, 2 * chips), z) for k in range(1, 2 * chips)]
+    line = [(dp, lax.rem(z + k, depth)) for k in range(1, depth)]
+    others = [(lax.rem(chip + k, chips) * 2 + core, z) for k in range(1, chips)]
+    sibling = (chip * 2 + 1 - core, z)
+    return dp, z, chip, core, group, line, others, sibling
+
+
+def feature_sum(value):
+    return jnp.sum(jnp.sum(value, axis=0), axis=1, keepdims=True)
+
+
+def norms(y, side, rows):
+    x = side[:, 0:rows, :]
+    post = side[:, rows : rows + 1, :]
+    final = side[:, rows + 1 : rows + 2, :]
+    rms_br = lax.rsqrt(feature_sum(y * y) / D + eps)[None]
+    stream = x + y * rms_br * post
+    rms_st = lax.rsqrt(feature_sum(stream * stream) / D + eps)[None]
+    return stream, rms_br, rms_st, post, final
+
+
+def branch_kernel(
+    chips, depth, h_ref, down_ref, x_ref, gains_ref, teacher_ref,
+    normed_ref, y_ref, side_ref, logits_ref,
+    side, part, got, total, sems,
+):
+    dp, z, chip, core, group, line, others, sibling = spots(chips, depth)
+    rows = x_ref.shape[2]
+    count = 2 * chips
+    half = chips
+    greet(group + line)
+    base = 0
+    sent = []
+    entries = logits_ref.shape[2]
+    tea = []
+    for k in range(1, depth):
+        cols = pl.ds(pl.multiple_of(lax.rem(z + k, depth) * entries, 128), entries)
+        tea.append(send(teacher_ref.at[:, cols], logits_ref.at[z], sems, base + k, line[k - 1]))
+    base += depth
+    for q in range(chips):
+        side[q, 0:rows, :] = x_ref[q, z].astype(jnp.float32)
+        side[q, rows : rows + 8, :] = gains_ref[...]
+    early = []
+    for k in range(1, count):
+        there = lax.rem(dp + k, count) // 2
+        early.append(send(side.at[there], side_ref.at[dp], sems, base + k, group[k - 1]))
+    base += count
+    side_ref[dp] = side[chip]
+    own = pl.ds(pl.multiple_of(z * entries, 128), entries)
+    logits_ref[z] = teacher_ref[:, own]
+    terms = jnp.dot(h_ref[...], down_ref[...], preferred_element_type=jnp.float32)
+    part[...] = terms.reshape(part.shape)
+    down = []
+    for k in range(1, depth):
+        there = lax.rem(z + k, depth)
+        down.append(send(part.at[:, there], got.at[k - 1], sems, base + k, line[k - 1]))
+    base += depth
+    for copy in down:
+        copy.wait_recv()
+    summed = part[:, z]
+    for k in range(1, depth):
+        summed += got[k - 1]
+    total[...] = summed
+    across = []
+    for k in range(1, count):
+        there = lax.rem(dp + k, count) // 2
+        across.append(send(total.at[there], y_ref.at[dp], sems, base + k, group[k - 1]))
+    base += count
+    y_ref[dp] = total[chip]
+    for copy in early + across:
+        copy.wait_recv()
+    stream, rms_br, rms_st, post, final = norms(y_ref[...], side_ref[...], rows)
+    normed_ref[:, chip, z] = (stream * rms_st * final).astype(jnp.bfloat16)
+    mine = pl.ds(core * half, half)
+    up = []
+    for k in range(1, depth):
+        block = normed_ref.at[mine, chip, z]
+        up.append(send(block, block, sems, base + k, line[k - 1]))
+    base += depth
+    wide = []
+    passed = []
+    for k in range(depth):
+        at = lax.rem(z + depth - k, depth)
+        block = normed_ref.at[mine, chip, at]
+        if k:
+            up[k - 1].wait_recv()
+            passed.append(send(block, block, sems, base + chips * depth + k, sibling))
+        for j in range(1, chips):
+            wide.append((j, send(block, block, sems, base + k * chips + j, others[j - 1])))
+    base += chips * depth + depth
+    for j in range(1, chips):
+        for other, copy in wide:
+            if other == j:
+                copy.wait_recv()
+        block = normed_ref.at[mine, lax.rem(chip + chips - j, chips)]
+        passed.append(send(block, block, sems, base + j, sibling))
+    for copy in passed + tea:
+        copy.wait_recv()
+    finish(tea + early + down + across + up + passed + [copy for _, copy in wide])
+
+
+def branch_forward(chips, depth, hidden, down_weight, x_blocks, gains, teacher_logits):
+    _, _, rows, features = x_blocks.shape
+    entries = teacher_logits.shape[1] // depth
+    count = 2 * chips
+    f32 = jnp.float32
+    return pl.pallas_call(
+        functools.partial(branch_kernel, chips, depth),
+        out_shape=(
+            jax.ShapeDtypeStruct((count, chips, depth, rows, features), jnp.bfloat16),
+            jax.ShapeDtypeStruct((count, rows, features), f32),
+            jax.ShapeDtypeStruct((count, rows + 8, features), f32),
+            jax.ShapeDtypeStruct((depth, teacher_logits.shape[0], entries), jnp.bfloat16),
+        ),
+        in_specs=[vmem()] * 5,
+        out_specs=(vmem(),) * 4,
+        scratch_shapes=[
+            pltpu.VMEM((chips, rows + 8, features), f32),
+            pltpu.VMEM((chips, depth, rows, features), f32),
+            pltpu.VMEM((depth - 1, chips, rows, features), f32),
+            pltpu.VMEM((chips, rows, features), f32),
+            pltpu.SemaphoreType.DMA((2, 4 * depth + 5 * chips + chips * depth)),
+        ],
+        compiler_params=pltpu.CompilerParams(
+            collective_id=3, has_side_effects=True, vmem_limit_bytes=48 * 2**20
+        ),
+    )(hidden, down_weight, x_blocks, gains, teacher_logits)
+
+
+def head_kernel(
+    chips, depth, normed_ref, emb_ref, teacher_ref, factor_ref, local_ref, y_ref, side_ref,
+    stats_ref, grad_emb_ref, dy_ref, back_ref,
+    student, exp_s, exp_t, flat, near, dp_stats, z_stats,
+    part, got_pair, out_chip, got_chip, line_part, got_line, owned, pay, sems,
+):
+    dp, z, chip, core, group, line, others, sibling = spots(chips, depth)
+    count = 2 * chips
+    half = chips
+    rows = y_ref.shape[1]
+    tokens, entries = teacher_ref.shape
+    f32, b16 = jnp.float32, jnp.bfloat16
+    greet(group + line)
+    raw = contract_last(normed_ref[0], emb_ref[0])
+    for d in range(1, count):
+        raw += contract_last(normed_ref[d], emb_ref[d])
+    logits = softcap_value * jnp.tanh(raw / softcap_value)
+    student[...] = logits
+    teacher = teacher_ref[...].astype(f32)
+    exp_s[...] = jnp.exp(logits)
+    exp_t[...] = jnp.exp(teacher)
+    hot = local_ref[...] == lax.broadcasted_iota(jnp.int32, (tokens, entries), 1)
+    lane = lax.broadcasted_iota(jnp.int32, (tokens, 128), 1)
+    sums = [
+        jnp.sum(exp_s[...], axis=1, keepdims=True),
+        jnp.sum(exp_t[...], axis=1, keepdims=True),
+        jnp.sum(exp_t[...] * (teacher - logits), axis=1, keepdims=True),
+        jnp.sum(jnp.where(hot, logits, 0.0), axis=1, keepdims=True),
+    ]
+    columns = jnp.zeros((tokens, 128), f32)
+    for i, value in enumerate(sums):
+        columns = jnp.where(lane == i, value, columns)
+    near[...] = columns.T[0:8, :]
+    base = 0
+    first = []
+    for k in range(1, count):
+        first.append(send(near, dp_stats.at[dp], sems, base + k, group[k - 1]))
+    base += count
+    dp_stats[dp] = near[...]
+    for copy in first:
+        copy.wait_recv()
+    z_stats[z] = jnp.sum(dp_stats[...], axis=0)
+    second = []
+    for k in range(1, depth):
+        second.append(send(z_stats.at[z], z_stats.at[z], sems, base + k, line[k - 1]))
+    base += depth
+    for copy in second:
+        copy.wait_recv()
+    whole = jnp.sum(z_stats[...], axis=0)
+    stats_ref[...] = whole
+    flat[...] = jnp.zeros_like(flat)
+    flat[0:8, :] = whole
+    columns = flat[...].T
+    total_s = columns[:, 0:1]
+    total_t = columns[:, 1:2]
+    capped = student[...] / softcap_value
+    dstudent = factor_ref[...] * (
+        exp_s[...] * ((1.0 + hard_weight) / total_s)
+        - exp_t[...] / total_t
+        - jnp.where(hot, hard_weight, 0.0)
+    )
+    dlogit = (dstudent * (1.0 - capped * capped)).astype(b16)
+    for d in range(count):
+        terms = jnp.dot(dlogit, emb_ref[d], preferred_element_type=f32)
+        part[d] = terms.astype(b16).reshape(chips, depth, rows, -1)
+    theirs = pl.ds((1 - core) * half, half)
+    mine = pl.ds(core * half, half)
+    order = list(range(1, chips)) + [0]
+    pair = {}
+    for k in order:
+        there = lax.rem(chip + k, chips)
+        pair[k] = send(part.at[theirs, there], got_pair.at[:, there], sems, base + k, sibling)
+    base += chips
+    far = []
+    for k in range(1, chips):
+        there = lax.rem(chip + k, chips)
+        pair[k].wait_recv()
+        for i in range(half):
+            out_chip[k - 1, i] = (
+                part[core * half + i, there].astype(f32) + got_pair[i, there].astype(f32)
+            ).astype(b16)
+        far.append(send(out_chip.at[k - 1], got_chip.at[k - 1], sems, base + k, others[k - 1]))
+    base += chips
+    for d in range(count):
+        grad_emb_ref[d] = contract_first(dlogit, normed_ref[d]).astype(b16)
+    pair[0].wait_recv()
+    for copy in far:
+        copy.wait_recv()
+    for i in range(half):
+        value = part[core * half + i, chip].astype(f32) + got_pair[i, chip].astype(f32)
+        for k in range(1, chips):
+            value += got_chip[k - 1, i].astype(f32)
+        line_part[:, i] = value.astype(b16)
+    across = []
+    for k in range(1, depth):
+        there = lax.rem(z + k, depth)
+        across.append(send(line_part.at[there], got_line.at[k - 1], sems, base + k, line[k - 1]))
+    base += depth
+    for copy in across:
+        copy.wait_recv()
+    value = line_part[z].astype(f32)
+    for k in range(1, depth):
+        value += got_line[k - 1].astype(f32)
+    owned[mine] = value
+    swap = send(owned.at[mine], owned.at[mine], sems, base, sibling)
+    base += 1
+    y = y_ref[...]
+    stream, rms_br, rms_st, post, final = norms(y, side_ref[...], rows)
+    swap.wait_recv()
+    along = owned[...] * final
+    mean_st = feature_sum(stream * along)[None] / D
+    dstream = rms_st * along - stream * (rms_st * rms_st * rms_st) * mean_st
+    back = dstream * post
+    mean_br = feature_sum(y * back)[None] / D
+    dbranch = rms_br * back - y * (rms_br * rms_br * rms_br) * mean_br
+    pay[:, 0] = dbranch.astype(b16)
+    pay[:, 1] = dstream.astype(b16)
+    home = []
+    for k in range(1, chips):
+        there = lax.rem(chip + k, chips) * 2 + core
+        home.append(send(pay.at[there], back_ref.at[chip], sems, base + k, others[k - 1]))
+    base += chips
+    back_ref[chip] = pay[dp]
+    for copy in home:
+        copy.wait_recv()
+    dy_ref[:, z] = back_ref[:, 0]
+    last = []
+    for k in range(1, depth):
+        last.append(send(dy_ref.at[:, z], dy_ref.at[:, z], sems, base + k, line[k - 1]))
+    for copy in last:
+        copy.wait_recv()
+    finish(first + second + list(pair.values()) + far + across + [swap] + home + last)
+
+
+def head_both(chips, depth, normed, emb_blocks, teacher, factor, local, y, side):
+    count, tokens, features = normed.shape
+    entries = emb_blocks.shape[1]
+    rows = y.shape[1]
+    f32, b16 = jnp.float32, jnp.bfloat16
+    return pl.pallas_call(
+        functools.partial(head_kernel, chips, depth),
+        out_shape=(
+            jax.ShapeDtypeStruct((8, tokens), f32),
+            jax.ShapeDtypeStruct((count, entries, features), b16),
+            jax.ShapeDtypeStruct((chips, depth, rows, features), b16),
+            jax.ShapeDtypeStruct((chips, 2, rows, features), b16),
+        ),
+        in_specs=[vmem()] * 7,
+        out_specs=(vmem(),) * 4,
+        scratch_shapes=[
+            pltpu.VMEM((tokens, entries), f32),
+            pltpu.VMEM((tokens, entries), f32),
+            pltpu.VMEM((tokens, entries), f32),
+            pltpu.VMEM((128, tokens), f32),
+            pltpu.VMEM((8, tokens), f32),
+            pltpu.VMEM((count, 8, tokens), f32),
+            pltpu.VMEM((depth, 8, tokens), f32),
+            pltpu.VMEM((count, chips, depth, rows, features), b16),
+            pltpu.VMEM((chips, chips, depth, rows, features), b16),
+            pltpu.VMEM((chips - 1, chips, depth, rows, features), b16),
+            pltpu.VMEM((chips - 1, chips, depth, rows, features), b16),
+            pltpu.VMEM((depth, chips, rows, features), b16),
+            pltpu.VMEM((depth - 1, chips, rows, features), b16),
+            pltpu.VMEM((count, rows, features), f32),
+            pltpu.VMEM((count, 2, rows, features), b16),
+            pltpu.SemaphoreType.DMA((2, 5 * chips + 3 * depth + 1)),
+        ],
+        compiler_params=pltpu.CompilerParams(
+            collective_id=4, has_side_effects=True, vmem_limit_bytes=48 * 2**20
+        ),
+    )(normed, emb_blocks, teacher, factor, local, y, side)
+
+
+def input_kernel(
+    chips, depth, dgate_ref, dup_ref, gate_ref, up_ref, x_ref, gain_ref, back_ref,
+    out_ref, part, got, scaled, mine, inner, sems,
+):
+    dp, z, chip, core, group, line, others, sibling = spots(chips, depth)
+    count = 2 * chips
+    f32, b16 = jnp.float32, jnp.bfloat16
+    rows = x_ref.shape[2]
+    greet(group + line)
+    dz = contract_last(dgate_ref[...], gate_ref[...]) + contract_last(dup_ref[...], up_ref[...])
+    part[...] = (dz * gain_ref[0:1, :]).astype(b16).reshape(part.shape)
+    base = 0
+    first = []
+    for k in range(1, depth):
+        there = lax.rem(z + k, depth)
+        first.append(send(part.at[:, there], got.at[k - 1], sems, base + k, line[k - 1]))
+    base += depth
+    for copy in first:
+        copy.wait_recv()
+    value = part[:, z].astype(f32)
+    for k in range(1, depth):
+        value += got[k - 1].astype(f32)
+    scaled[...] = value
+    x = x_ref[:, z].astype(f32)
+    lane = lax.broadcasted_iota(jnp.int32, (chips, rows, 128), 2)
+    products = jnp.sum(x * value, axis=2, keepdims=True)
+    squares = jnp.sum(x * x, axis=2, keepdims=True)
+    mine[...] = jnp.where(lane == 0, products, jnp.where(lane == 1, squares, 0.0))
+    second = []
+    for k in range(1, count):
+        second.append(send(mine, inner.at[dp], sems, base + k, group[k - 1]))
+    base += count
+    inner[dp] = mine[...]
+    for copy in second:
+        copy.wait_recv()
+    sums = jnp.sum(inner[...], axis=0)
+    mean = sums[:, :, 0:1] / D / (sums[:, :, 1:2] / D + eps)
+    out_ref[:, z] = (back_ref[:, 1].astype(f32) + scaled[...] - x * mean).astype(b16)
+    last = []
+    for k in range(1, depth):
+        last.append(send(out_ref.at[:, z], out_ref.at[:, z], sems, base + k, line[k - 1]))
+    for copy in last:
+        copy.wait_recv()
+    finish(first + second + last)
+
+
+def input_backward(chips, depth, dgate, dup, gate_weight, up_weight, x_blocks, gain, back):
+    _, _, rows, features = x_blocks.shape
+    f32, b16 = jnp.float32, jnp.bfloat16
+    return pl.pallas_call(
+        functools.partial(input_kernel, chips, depth),
+        out_shape=jax.ShapeDtypeStruct((chips, depth, rows, features), b16),
+        in_specs=[vmem()] * 7,
+        out_specs=vmem(),
+        scratch_shapes=[
+            pltpu.VMEM((chips, depth, rows, features), b16),
+            pltpu.VMEM((depth - 1, chips, rows, features), b16),
+            pltpu.VMEM((chips, rows, features), f32),
+            pltpu.VMEM((chips, rows, 128), f32),
+            pltpu.VMEM((2 * chips, chips, rows, 128), f32),
+            pltpu.SemaphoreType.DMA((2, 2 * depth + 2 * chips)),
+        ],
+        compiler_params=pltpu.CompilerParams(
+            collective_id=5, has_side_effects=True, vmem_limit_bytes=48 * 2**20
+        ),
+    )(dgate, dup, gate_weight, up_weight, x_blocks, gain, back)
+
+
 def on_device(
     chips,
+    depth,
     hidden_in,
     pre_gain,
     gate_weight,
@@ -358,7 +733,8 @@
     target_ids,
     lengths,
 ):
-    positions = hidden_in.shape[0]
+    positions, features = hidden_in.shape
+    rows = positions // (chips * depth)
     xf = hidden_in.astype(jnp.float32)
     x_gained = (xf * pre_gain).astype(jnp.bfloat16)
     square_local = jnp.sum(xf * xf, axis=1)
@@ -370,81 +746,59 @@
         up_weight,
     )
     hidden = h_blocks.reshape(positions, -1)
-    branch = lax.psum(jnp.dot(hidden, down_weight, preferred_element_type=jnp.float32), "vocab")
-    gained = branch * post_gain
-    square_br = lax.psum(jnp.sum(branch * branch, axis=1), "dp")
-    rms_br = lax.rsqrt(square_br / D + eps)[:, None]
-    stream = xf + gained * rms_br
-    square_st = lax.psum(jnp.sum(stream * stream, axis=1), "dp")
-    rms_st = lax.rsqrt(square_st / D + eps)[:, None]
-    normed_local = (stream * rms_st * final_gain).astype(jnp.bfloat16)
-    normed = lax.all_gather(normed_local, "dp", axis=1, tiled=True)
-    raw = contract_last(normed, embedding)
-    student = softcap_value * jnp.tanh(raw / softcap_value)
-    teacher = lax.all_to_all(
-        teacher_logits, "vocab", split_axis=1, concat_axis=0, tiled=True
-    ).astype(jnp.float32)
+    x_blocks = hidden_in.reshape(chips, depth, rows, features)
+    gains = jnp.pad(jnp.stack([post_gain, final_gain]), ((0, 6), (0, 0)))
+    normed, y, side, teacher = branch_forward(
+        chips, depth, hidden, down_weight, x_blocks, gains, teacher_logits
+    )
     entries = embedding.shape[0]
-    columns = lax.axis_index(("dp", "vocab")) * entries + jnp.arange(entries, dtype=jnp.int32)
-    onehot = jnp.where(target_ids[:, None] == columns[None, :], 1.0, 0.0).astype(jnp.float32)
-    exp_s = jnp.exp(student)
-    exp_t = jnp.exp(teacher)
-    total_s, total_t, weighted, picked = lax.psum(
-        (
-            jnp.sum(exp_s, axis=1),
-            jnp.sum(exp_t, axis=1),
-            jnp.sum(exp_t * (teacher - student), axis=1),
-            jnp.sum(onehot * student, axis=1),
-        ),
-        ("dp", "vocab"),
-    )
+    mask = token_mask(lengths, positions)
+    count = jnp.sum(lengths).astype(jnp.float32)
+    first_entry = lax.axis_index(("dp", "vocab")) * entries
+    emb_blocks = embedding.reshape(entries, 2 * chips, features).transpose(1, 0, 2)
+    stats, grad_emb, dy_blocks, back = head_both(
+        chips,
+        depth,
+        normed.reshape(2 * chips, positions, features),
+        emb_blocks,
+        teacher.reshape(positions, entries),
+        (loss_scale / count * mask)[:, None],
+        (target_ids - first_entry)[:, None],
+        y,
+        side,
+    )
+    total_s, total_t, weighted, picked = stats[0], stats[1], stats[2], stats[3]
     log_s = jnp.log(total_s)
     log_t = jnp.log(total_t)
-    mask = token_mask(lengths, positions)
-    count = jnp.sum(lengths).astype(jnp.float32)
     per_token = weighted / total_t - log_t + log_s + hard_weight * (log_s - picked)
     loss = jnp.sum(mask * per_token) / count
-    factor = loss_scale / count * mask[:, None]
-    dstudent = factor * (
-        (1.0 + hard_weight) * exp_s / total_s[:, None]
-        - exp_t / total_t[:, None]
-        - hard_weight * onehot
-    )
-    capped = student / softcap_value
-    dlogit = (dstudent * (1.0 - capped * capped)).astype(jnp.bfloat16)
-    grad_embedding = contract_first(dlogit, normed).astype(jnp.bfloat16)
-    partial_grad = jnp.dot(dlogit, embedding, preferred_element_type=jnp.float32)
-    local_grad = lax.psum_scatter(partial_grad, "dp", scatter_dimension=1, tiled=True)
-    dnormed = lax.psum(local_grad, "vocab")
-    along = dnormed * final_gain
-    cube_st = rms_st * rms_st * rms_st
-    cube_br = rms_br * rms_br * rms_br
-    stream_along = lax.psum(jnp.sum(stream * along, axis=1), "dp")
-    dstream = rms_st * along - stream * cube_st * (stream_along[:, None] / D)
-    back = dstream * post_gain
-    branch_back = lax.psum(jnp.sum(branch * back, axis=1), "dp")
-    mean_br = branch_back[:, None] / D
-    dbranch = rms_br * back - branch * cube_br * mean_br
-    grad_out = dbranch.astype(jnp.bfloat16)
+    grad_embedding = grad_emb.transpose(1, 0, 2).reshape(entries, -1)
+    grad_out = dy_blocks.reshape(positions, features)
     pairs = hidden_backward(chips, grad_out, down_weight, act, slope)
     dgate = pairs[:, :, 0].reshape(positions, -1)
     dup = pairs[:, :, 1].reshape(positions, -1)
     grad_down = contract_first(hidden, grad_out).astype(jnp.bfloat16)
     grad_gate = contract_first(x_gained, dgate).astype(jnp.bfloat16)
     grad_up = contract_first(x_gained, dup).astype(jnp.bfloat16)
-    dz = lax.psum(contract_last(dgate, gate_weight) + contract_last(dup, up_weight), "vocab")
-    scaled = dz * pre_gain
-    input_inner, square_in = lax.psum((jnp.sum(xf * scaled, axis=1), square_local), "dp")
-    mean_in = 1.0 / (square_in / D + eps) * (input_inner / D)
-    grad_hidden = (dstream + scaled - xf * mean_in[:, None]).astype(jnp.bfloat16)
+    gain = jnp.broadcast_to(pre_gain[None, :], (8, features))
+    grad_hidden = input_backward(
+        chips, depth, dgate, dup, gate_weight, up_weight, x_blocks, gain, back
+    ).reshape(positions, features)
     return (loss, grad_hidden, grad_gate, grad_up, grad_down, grad_embedding)
 
 
 def pick_plan(mesh):
     chips = mesh.shape["dp"] // 2
+    depth = mesh.shape["vocab"]
     tokens = LENGTH * 2
-    if mesh.shape["dp"] % 2 == 0 and chips > 1 and tokens % (32 * chips) == 0:
-        return functools.partial(on_device, chips)
+    if (
+        mesh.shape["dp"] % 2 == 0
+        and chips > 1
+        and depth > 1
+        and tokens % (32 * chips) == 0
+        and tokens % (16 * chips * depth) == 0
+    ):
+        return functools.partial(on_device, chips, depth)
     return on_device_plain
 
 

time: 440 us -> 255 us (0.58)
  waiting for transfers between devices: 162 us -> 0 us
  Pallas kernels: 92.2 us -> 209 us
  blocking collectives: 103 us -> 0 us
  other arithmetic: 18.2 us -> 2.23 us
  matrix products: 24.1 us -> 9.66 us
  between operations: 16.5 us -> 3.35 us
  local copies, waits for them, and re-layouts: 19.6 us -> 29.7 us
    pallas_call x0 -> x3, Pallas kernels: none -> 117 us  [the longest x1 47 us: head_both(): pl.pallas_call(functools.partial(head_kernel, chips, depth), out_shape=(j...]
    psum x6 -> x0, blocking collectives: 103 us -> none  [the longest x1 39.3 us: on_device(): lax.psum((jnp.sum(exp_s, axis=1), jnp.sum(exp_t, axis=1), jnp.sum(exp_t *...]
    psum x3 -> x0, waiting for transfers between devices: 97.5 us -> none  [the longest x1 38.9 us: on_device(): lax.psum(jnp.dot(hidden, down_weight, preferred_element_type=jnp.float32)...]
    unnamed x6 -> x0, waiting for transfers between devices: 49.7 us -> none
    all_gather x1 -> x0, waiting for transfers between devices: 11.7 us -> none  [on_device(): normed = lax.all_gather(normed_local, 'dp', axis=1, tiled=True)]
    unnamed x55 -> x43, local copies, waits for them, and re-layouts: 14.6 us -> 22.8 us
    reduce_sum x6 -> x1, other arithmetic: 7.8 us -> 0.6 us  [on_device(): loss = jnp.sum(mask * per_token) / count]
    dot_general x4 -> x0, matrix products: 6.86 us -> none  [the longest x3 4.94 us: contract_last(): lax.dot_general(left, right, (((1,), (1,)), ((), ())), preferred_element_...]
  transfers between devices with their start and end apart: 6 -> 0, of which waited for: 6 -> 0; matrix products, arithmetic and copies ran while one was open for 5% -> 0% of each run, Pallas kernels for 0% -> 0%
where the time goes in v2:
time: 255 us; the launch traced here: 254 us
  Pallas kernels  209 us (82%)
  local copies, waits for them, and re-layouts  29.7 us (12%)
  matrix products  9.66 us (4%)
  between operations  3.35 us (1%)
    pallas_call x1, Pallas kernels, ffn_forward(): pl.pallas_call(functools.partial(ffn_kernel, chips, rows), out_shape=(jax...  50.4 us
    pallas_call x1, Pallas kernels, head_both(): pl.pallas_call(functools.partial(head_kernel, chips, depth), out_shape=(j...  47 us
    pallas_call x1, Pallas kernels, branch_forward(): pl.pallas_call(functools.partial(branch_kernel, chips, depth), out_shape=...  43.6 us
    pallas_call x1, Pallas kernels, hidden_backward(): pl.pallas_call(functools.partial(hidden_kernel, chips, rows), out_shape=j...  41.4 us
    pallas_call x1, Pallas kernels, input_backward(): pl.pallas_call(functools.partial(input_kernel, chips, depth), out_shape=j...  26.5 us
    unnamed x43, local copies, waits for them, and re-layouts  22.8 us
    dot_general x3, matrix products, contract_first(): lax.dot_general(left, right, (((0,), (0,)), ((), ())), preferred_element_...  9.66 us

profile of v2, /device:TPU:0, one launch (start us, length us, event | category | flops | bytes accessed | tf_op | source)
XLA Modules:
  0.0 253.9 jit_solution(16702995005681045538)
XLA Ops:
  0.6 1.1 copy.33
  1.7 0.8 fusion.1
  2.6 0.1 broadcast_in_dim.48.square_ref
  2.7 50.4 %shard_map.154 = (bf16[4,2,32,3584]{3,2,1,0:T(8,128)(2,1)S(1)}, f32[32,3584]{1,0:T(8,128)S(1)}, f32[32,3584]{1,0:T(8,128)S(1)}) custom-call(bf16[256,448]{1,0:T(8,128)(2,1)S(1)} %get-tuple-element.49.x_ref, f32[256,128]{1,0:T(8,128)S(1)} %broadcast_in_dim.48.square_ref, bf16[448,3584]{1,0:T(8,128)(2,1)} %gate_ref.3, bf16[448,3584]{1,0:T(8,128)(2,1)} %up_ref.3), custom_call_target="tpu_custom_call" | custom-call | tf_op jit(solution)/shard_map/pallas_call | solution.py:278
  53.1 0.0 copy-start.1
  53.1 0.0 copy-start.15
  53.1 0.0 copy-start.16
  53.1 6.4 %copy.35.down_ref = bf16[3584,448]{1,0:T(8,128)(2,1)} copy(bf16[3584,448]{0,1:T(8,128)(2,1)} %param.15) | data formatting | bytes 6422528 | tf_op args[4]
  59.5 0.0 copy-done.15
  59.5 0.0 copy-done.16
  59.5 0.0 copy-done.1
  59.5 0.0 copy-start.11
  59.5 0.9 copy-done.11
  60.4 43.6 %shard_map.155 = (bf16[8,4,4,16,448]{4,3,2,1,0:T(8,128)(2,1)S(1)}, f32[8,16,448]{2,1,0:T(8,128)S(1)}, f32[8,24,448]{2,1,0:T(8,128)S(1)}, bf16[4,64,256]{2,1,0:T(8,128)(2,1)S(1)}) custom-call(bf16[256,3584]{1,0:T(8,128)(2,1)S(1)} %bitcast.27, bf16[3584,448]{1,0:T(8,128)(2,1)} %copy.35.down_ref, bf16[4,4,16,448]{3,2,1,0:T(8,128)(2,1)S(1)} %bitcast.29, ...), custom_call_target="tpu_custom_call" | custom-call | tf_op jit(solution)/shard_map/pallas_call | solution.py:457
  104.0 0.0 copy-start.3
  104.1 1.3 copy-done.3
  105.4 0.7 copy-done.7
  106.1 0.7 copy-done.12
  106.8 0.0 copy-done.18
  106.8 0.1 fusion.6
  106.9 0.1 copy.38
  107.0 0.6 reduce_sum.40
  108.4 0.0 copy-done.17
  108.4 0.1 copy.39.local_ref
  108.5 3.8 %copy.36 = bf16[256,3584]{0,1:T(8,128)(2,1)} copy(bf16[256,3584]{1,0:T(8,128)(2,1)} %param.18) | data formatting | bytes 3670016 | tf_op args[7]
  112.3 0.0 copy-done.9
  112.4 0.0 copy-start.10
  112.4 3.9 %copy.37 = bf16[256,8,448]{2,0,1:T(8,128)(2,1)} copy(bf16[256,8,448]{0,2,1:T(8,128)(2,1)} %bitcast.39) | data formatting | bytes 3670016 | tf_op jit(solution)/shard_map/reshape | solution.py:758
  116.2 0.0 copy-done.8
  116.3 0.0 copy-start.4
  116.3 1.6 copy-done.4
  117.9 47.0 %shard_map.156 = (f32[8,256]{1,0:T(8,128)S(1)}, bf16[8,256,448]{2,1,0:T(8,128)(2,1)S(1)}, bf16[4,4,16,448]{3,2,1,0:T(8,128)(2,1)S(1)}, bf16[4,2,16,448]{3,2,1,0:T(8,128)(2,1)S(1)}) custom-call(bf16[8,256,448]{2,1,0:T(8,128)(2,1)S(1)} %bitcast.31, bf16[8,256,448]{2,1,0:T(8,128)(2,1)} %bitcast.37, bf16[256,256]{1,0:T(8,128)(2,1)S(1)} %bitcast.36, ...), custom_call_target="tpu_custom_call" | custom-call | tf_op jit(solution)/shard_map/pallas_call | solution.py:619
  164.9 0.0 copy-start.5
  164.9 1.3 copy-done.5
  166.2 41.4 %shard_map.157 = bf16[4,2,2,32,3584]{4,3,2,1,0:T(8,128)(2,1)S(1)} custom-call(bf16[256,448]{1,0:T(8,128)(2,1)S(1)} %bitcast.33, bf16[3584,448]{1,0:T(8,128)(2,1)} %copy.35.down_ref, f32[32,3584]{1,0:T(8,128)S(1)} %get-tuple-element.24.act_ref, f32[32,3584]{1,0:T(8,128)S(1)} %get-tuple-element.25.slope_ref), custom_call_target="tpu_custom_call" | custom-call | tf_op jit(solution)/shard_map/pallas_call | solution.py:329
  207.6 0.0 copy-start.14
  207.6 0.3 fusion.10
  207.9 0.0 copy-start
  207.9 0.3 copy-done.14
  208.3 26.5 %shard_map.158 = bf16[4,4,16,448]{3,2,1,0:T(8,128)(2,1)S(1)} custom-call(bf16[256,3584]{1,0:T(8,128)(2,1)S(1)} %bitcast.23, bf16[256,3584]{1,0:T(8,128)(2,1)S(1)} %bitcast.25, bf16[448,3584]{1,0:T(8,128)(2,1)} %gate_ref.3, bf16[448,3584]{1,0:T(8,128)(2,1)} %up_ref.3, bf16[4,4,16,448]{3,2,1,0:T(8,128)(2,1)S(1)} %bitcast.30, ...), custom_call_target="tpu_custom_call" | custom-call | tf_op jit(solution)/shard_map/pallas_call | solution.py:702
  234.8 0.0 copy-done
  234.8 0.8 copy.42
  235.6 4.2 %convolution_convert_fusion.1 = bf16[448,3584]{1,0:T(8,128)(2,1)} fusion(bf16[256,448]{1,0:T(8,128)(2,1)S(1)} %get-tuple-element.49.x_ref, bf16[256,3584]{1,0:T(8,128)(2,1)} %bitcast.26), kind=kOutput, calls=%fused_computation.1 | convolution fusion | flops 823689216 | bytes 5275648 | tf_op jit(solution)/shard_map/dot_general | solution.py:39
  239.8 2.7 %convolution_convert_fusion.2 = bf16[448,3584]{1,0:T(8,128)(2,1)} fusion(bf16[256,448]{1,0:T(8,128)(2,1)S(1)} %get-tuple-element.49.x_ref, bf16[256,3584]{1,0:T(8,128)(2,1)S(1)} %bitcast.24), kind=kOutput, calls=%fused_computation.2 | convolution fusion | flops 823689216 | bytes 5275648 | tf_op jit(solution)/shard_map/dot_general | solution.py:39
  242.6 2.7 %convolution_convert_fusion = bf16[3584,448]{0,1:T(8,128)(2,1)} fusion(bf16[256,3584]{1,0:T(8,128)(2,1)S(1)} %bitcast.28, bf16[256,448]{1,0:T(8,128)(2,1)S(1)} %bitcast.34), kind=kOutput, calls=%fused_computation | convolution fusion | flops 823689216 | bytes 5275648 | tf_op jit(solution)/shard_map/dot_general | solution.py:39
  245.3 0.6 fusion.9
  246.6 2.3 copy.41
  248.9 3.8 %copy.43 = bf16[256,3584]{1,0:T(8,128)(2,1)} copy(bf16[256,3584]{0,1:T(8,128)(2,1)} %bitcast.38) | data formatting | bytes 3670016
  (19 shorter events, 0.1 us)
Async XLA Ops:
  53.1 6.4 %copy-start.1 = (bf16[4,2,32,3584]{3,2,1,0:T(8,128)(2,1)}, bf16[4,2,32,3584]{3,2,1,0:T(8,128)(2,1)S(1)}, u32[]{:S(2)}) copy-start(bf16[4,2,32,3584]{3,2,1,0:T(8,128)(2,1)S(1)} %get-tuple-element.17) | copy-start | bytes 5505028
  53.1 6.4 %copy-start.15 = (f32[448]{0:T(512)S(1)}, f32[448]{0:T(512)}, u32[]{:S(2)}) copy-start(f32[448]{0:T(512)} %param.17) | copy-start | bytes 5380
  53.1 6.4 %copy-start.16 = (f32[448]{0:T(512)S(1)}, f32[448]{0:T(512)}, u32[]{:S(2)}) copy-start(f32[448]{0:T(512)} %param.16) | copy-start | bytes 5380
  59.5 0.9 copy-start.11
  60.4 46.4 %copy-start.18 = (s32[2]{0:T(128)S(1)}, s32[2]{0:T(128)}, u32[]{:S(2)}) copy-start(s32[2]{0:T(128)} %param.21) | copy-start | bytes 28
  60.4 48.0 %copy-start.17 = (s32[256]{0:T(256)S(1)}, s32[256]{0:T(256)}, u32[]{:S(2)}) copy-start(s32[256]{0:T(256)} %param.20) | copy-start | bytes 3076
  104.0 1.3 copy-start.3
  105.4 0.7 copy-start.7
  106.1 0.7 copy-start.12
  106.8 5.6 %copy-start.9 = (f32[8,16,448]{2,1,0:T(8,128)}, f32[8,16,448]{2,1,0:T(8,128)S(1)}, u32[]{:S(2)}) copy-start(f32[8,16,448]{2,1,0:T(8,128)S(1)} %get-tuple-element.20.y_ref) | copy-start | bytes 688132
  112.3 3.9 %copy-start.8 = (f32[8,24,448]{2,1,0:T(8,128)S(1)}, f32[8,24,448]{2,1,0:T(8,128)}, u32[]{:S(2)}) copy-start(f32[8,24,448]{2,1,0:T(8,128)} %copy-done.7) | copy-start | bytes 1032196
  112.3 3.9 %copy-start.13 = (bf16[4,64,256]{2,1,0:T(8,128)(2,1)S(1)}, bf16[4,64,256]{2,1,0:T(8,128)(2,1)}, u32[]{:S(2)}) copy-start(bf16[4,64,256]{2,1,0:T(8,128)(2,1)} %copy-done.12) | copy-start | bytes 393220
  112.4 3.9 %copy-start.10 = (f32[8,16,448]{2,1,0:T(8,128)S(1)}, f32[8,16,448]{2,1,0:T(8,128)}, u32[]{:S(2)}) copy-start(f32[8,16,448]{2,1,0:T(8,128)} %copy-done.9) | copy-start | bytes 688132
  116.3 1.6 copy-start.4
  164.9 1.3 copy-start.5
  207.6 0.7 copy-start.14
  207.9 26.9 %copy-start = (bf16[4,2,1,32,3584]{4,3,2,1,0:T(8,128)(2,1)}, bf16[4,2,1,32,3584]{4,3,2,1,0:T(8,128)(2,1)S(1)}, u32[]{:S(2)}) copy-start(bf16[4,2,1,32,3584]{4,3,2,1,0:T(8,128)(2,1)S(1)} %get-tuple-element.46) | copy-start | bytes 5505028
  239.8 2.7 %copy-start.2 = (bf16[4,2,32,3584]{3,2,1,0:T(8,128)(2,1)S(1)}, bf16[4,2,32,3584]{3,2,1,0:T(8,128)(2,1)}, u32[]{:S(2)}) copy-start(bf16[4,2,32,3584]{3,2,1,0:T(8,128)(2,1)} %copy-done.1) | copy-start | bytes 5505028
  242.6 4.0 %copy-start.6 = (bf16[8,256,448]{2,1,0:T(8,128)(2,1)S(1)}, bf16[8,256,448]{2,1,0:T(8,128)(2,1)}, u32[]{:S(2)}) copy-start(bf16[8,256,448]{2,1,0:T(8,128)(2,1)} %copy-done.5) | copy-start | bytes 5505028

commit v3 on v2

--- a/solution.py
+++ b/solution.py
@@ -139,7 +139,7 @@
 MESH_ID = pl.DeviceIdType.MESH
 CUBE = 0.044715
 ROOT = 0.7978845608028654
-TILE = 512
+PIECES = 4
 
 
 def vmem():
@@ -175,60 +175,61 @@
     return chip, core, sibling, others
 
 
-def scatter_sum(chips, part, got_pair, out_chip, got_chip, sems, base):
+def scatter_start(chips, part, got_pair, sems, base):
     chip, core, sibling, others = places(chips)
-    order = list(range(1, chips)) + [0]
     pair = {}
-    for k in order:
+    for k in list(range(1, chips)) + [0]:
         there = (chip + k) % chips
         pair[k] = send(part.at[there, 1 - core], got_pair.at[there], sems, base + k, sibling)
-    far = {}
-    width = part.shape[-1]
-    step = min(TILE, width)
-    for k in order:
+    return pair
+
+
+def scatter_chips(chips, pair, part, got_pair, out_chip, got_chip, sems, base):
+    chip, core, sibling, others = places(chips)
+    far = []
+    for k in range(1, chips):
         there = (chip + k) % chips
         pair[k].wait_recv()
-        if k:
-            for at in range(0, width, step):
-                cols = pl.ds(at, step)
-                total = part[there, core, :, cols].astype(jnp.float32) + got_pair[
-                    there, :, cols
-                ].astype(jnp.float32)
-                out_chip[k - 1, :, cols] = total.astype(out_chip.dtype)
-            far[k] = send(
-                out_chip.at[k - 1], got_chip.at[k - 1], sems, base + chips + k, others[k - 1]
-            )
-    for k in range(1, chips):
-        far[k].wait_recv()
-
-    def take(rows, cols):
-        total = part[chip, core, rows, cols].astype(jnp.float32) + got_pair[
-            chip, rows, cols
-        ].astype(jnp.float32)
+        total = part[there, core].astype(jnp.float32) + got_pair[there].astype(jnp.float32)
+        out_chip[k - 1] = total.astype(out_chip.dtype)
+        far.append(
+            send(out_chip.at[k - 1], got_chip.at[k - 1], sems, base + chips + k, others[k - 1])
+        )
+    return far
+
+
+def scatter_end(chips, pair, far, part, got_pair, got_chip):
+    chip, core, sibling, others = places(chips)
+    pair[0].wait_recv()
+    for copy in far:
+        copy.wait_recv()
+
+    def take(rows):
+        total = part[chip, core, rows].astype(jnp.float32) + got_pair[chip, rows].astype(
+            jnp.float32
+        )
         for k in range(1, chips):
-            total += got_chip[k - 1, rows, cols].astype(jnp.float32)
+            total += got_chip[k - 1, rows].astype(jnp.float32)
         return total
 
-    return take, list(pair.values()) + list(far.values())
-
-
-def gather_blocks(chips, out, sems, base):
+    return take
+
+
+def gather_start(chips, out, cols, sems, base):
     chip, core, sibling, others = places(chips)
-    mine = out.at[chip, core]
-    sent = [
-        send(mine, mine, sems, base + k, others[k - 1]) for k in range(1, chips)
-    ]
-    near = send(mine, mine, sems, base, sibling)
+    mine = out.at[(chip, core) + cols]
+    sent = [send(mine, mine, sems, base + k, others[k - 1]) for k in range(1, chips)]
+    return sent, send(mine, mine, sems, base, sibling)
+
+
+def gather_pass(chips, out, cols, sent, sems, base):
+    chip, core, sibling, others = places(chips)
     passed = []
     for k in range(1, chips):
         sent[k - 1].wait_recv()
-        origin = (chip + chips - k) % chips
-        block = out.at[origin, core]
+        block = out.at[((chip + chips - k) % chips, core) + cols]
         passed.append(send(block, block, sems, base + chips + k, sibling))
-    near.wait_recv()
-    for copy in passed:
-        copy.wait_recv()
-    return sent + [near] + passed
+    return passed
 
 
 def finish(copies):
@@ -243,37 +244,69 @@
 ):
     chip, core, sibling, others = places(chips)
     greet([sibling] + others)
-    ff = gate_ref.shape[1]
+    cut = part.shape[-1]
+    pieces = part.shape[0]
     sq[...] = square_ref[...].reshape(sq.shape)
-    for at in range(0, ff, TILE):
-        cols = pl.ds(at, TILE)
+    top = 4 * chips * pieces
+    pair_sq = scatter_start(chips, sq, sq_pair, sems, top)
+    pairs = []
+    for i in range(pieces):
         for which, weight in ((0, gate_ref), (1, up_ref)):
-            terms = jnp.dot(x_ref[...], weight[:, cols], preferred_element_type=jnp.float32)
-            part[:, :, pl.ds(which * rows, rows), cols] = terms.astype(jnp.bfloat16).reshape(
-                chips, 2, rows, TILE
+            terms = jnp.dot(
+                x_ref[...], weight[:, pl.ds(i * cut, cut)], preferred_element_type=jnp.float32
             )
-    take_sq, sent_sq = scatter_sum(chips, sq, sq_pair, sq_out, sq_chip, sems, 0)
-    take, sent = scatter_sum(chips, part, got_pair, out_chip, got_chip, sems, 2 * chips)
-    rms = lax.rsqrt(take_sq(pl.ds(0, rows), pl.ds(0, 128))[:, :1] / D + eps)
-    for at in range(0, ff, TILE):
-        cols = pl.ds(at, TILE)
-        gate = take(pl.ds(0, rows), cols) * rms
-        up = take(pl.ds(rows, rows), cols) * rms
+            part[i, :, :, pl.ds(which * rows, rows), :] = terms.astype(jnp.bfloat16).reshape(
+                chips, 2, rows, cut
+            )
+        pairs.append(
+            scatter_start(chips, part.at[i], got_pair.at[i], sems, 4 * chips * i)
+        )
+    far_sq = scatter_chips(chips, pair_sq, sq, sq_pair, sq_out, sq_chip, sems, top)
+    fars = []
+    for i in range(pieces):
+        fars.append(
+            scatter_chips(
+                chips, pairs[i], part.at[i], got_pair.at[i], out_chip.at[i], got_chip.at[i],
+                sems, 4 * chips * i,
+            )
+        )
+    take_sq = scatter_end(chips, pair_sq, far_sq, sq, sq_pair, sq_chip)
+    rms = lax.rsqrt(take_sq(pl.ds(0, rows))[:, :1] / D + eps)
+    copies = list(pair_sq.values()) + far_sq
+    gathers = []
+    for i in range(pieces):
+        cols = pl.ds(i * cut, cut)
+        take = scatter_end(chips, pairs[i], fars[i], part.at[i], got_pair.at[i], got_chip.at[i])
+        gate = take(pl.ds(0, rows)) * rms
+        up = take(pl.ds(rows, rows)) * rms
         square = gate * gate
         bend = jnp.tanh(ROOT * (gate + CUBE * gate * square))
         half = 0.5 * (1.0 + bend)
         act = gate * half
         slope = half + 0.5 * gate * (1.0 - bend * bend) * (ROOT * (1.0 + 3.0 * CUBE * square))
         h_ref[chip, core, :, cols] = (act * up).astype(jnp.bfloat16)
+        gathers.append(
+            gather_start(chips, h_ref, (slice(None), cols), sems, 4 * chips * i + 2 * chips)
+        )
         act_ref[:, cols] = act * rms
         slope_ref[:, cols] = up * slope * rms
-    finish(sent_sq + sent + gather_blocks(chips, h_ref, sems, 4 * chips))
+        copies += list(pairs[i].values()) + fars[i]
+    for i in range(pieces):
+        cols = (slice(None), pl.ds(i * cut, cut))
+        sent, near = gathers[i]
+        passed = gather_pass(chips, h_ref, cols, sent, sems, 4 * chips * i + 2 * chips)
+        for copy in [near] + passed:
+            copy.wait_recv()
+        copies += sent + [near] + passed
+    finish(copies)
 
 
 def ffn_forward(chips, x_gained, squares, gate_weight, up_weight):
     tokens = x_gained.shape[0]
     ff = gate_weight.shape[1]
     rows = tokens // (2 * chips)
+    pieces = PIECES if ff % (128 * PIECES) == 0 else 1
+    cut = ff // pieces
     b16, f32 = jnp.bfloat16, jnp.float32
     return pl.pallas_call(
         functools.partial(ffn_kernel, chips, rows),
@@ -285,15 +318,15 @@
         in_specs=[vmem()] * 4,
         out_specs=(vmem(),) * 3,
         scratch_shapes=[
-            pltpu.VMEM((chips, 2, 2 * rows, ff), b16),
-            pltpu.VMEM((chips, 2 * rows, ff), b16),
-            pltpu.VMEM((chips - 1, 2 * rows, ff), b16),
-            pltpu.VMEM((chips - 1, 2 * rows, ff), b16),
+            pltpu.VMEM((pieces, chips, 2, 2 * rows, cut), b16),
+            pltpu.VMEM((pieces, chips, 2 * rows, cut), b16),
+            pltpu.VMEM((pieces, chips - 1, 2 * rows, cut), b16),
+            pltpu.VMEM((pieces, chips - 1, 2 * rows, cut), b16),
             pltpu.VMEM((chips, 2, rows, 128), f32),
             pltpu.VMEM((chips, rows, 128), f32),
             pltpu.VMEM((chips - 1, rows, 128), f32),
             pltpu.VMEM((chips - 1, rows, 128), f32),
-            pltpu.SemaphoreType.DMA((2, 6 * chips)),
+            pltpu.SemaphoreType.DMA((2, 4 * chips * pieces + 2 * chips)),
         ],
         compiler_params=pltpu.CompilerParams(
             collective_id=1, has_side_effects=True, vmem_limit_bytes=48 * 2**20
@@ -307,24 +340,55 @@
 ):
     chip, core, sibling, others = places(chips)
     greet([sibling] + others)
-    ff = down_ref.shape[0]
-    for at in range(0, ff, TILE):
-        cols = pl.ds(at, TILE)
-        terms = contract_last(dy_ref[...], down_ref[cols, :])
-        part[:, :, :, cols] = terms.astype(jnp.bfloat16).reshape(chips, 2, rows, TILE)
-    take, sent = scatter_sum(chips, part, got_pair, out_chip, got_chip, sems, 0)
-    for at in range(0, ff, TILE):
-        cols = pl.ds(at, TILE)
-        dh = take(pl.ds(0, rows), cols)
+    cut = part.shape[-1]
+    pieces = part.shape[0]
+    pairs = []
+    for i in range(pieces):
+        terms = jnp.dot(
+            dy_ref[...], down_ref[:, pl.ds(i * cut, cut)], preferred_element_type=jnp.float32
+        )
+        part[i] = terms.astype(jnp.bfloat16).reshape(chips, 2, rows, cut)
+        pairs.append(
+            scatter_start(chips, part.at[i], got_pair.at[i], sems, 4 * chips * i)
+        )
+    fars = []
+    for i in range(pieces):
+        fars.append(
+            scatter_chips(
+                chips, pairs[i], part.at[i], got_pair.at[i], out_chip.at[i], got_chip.at[i],
+                sems, 4 * chips * i,
+            )
+        )
+    copies = []
+    gathers = []
+    for i in range(pieces):
+        cols = pl.ds(i * cut, cut)
+        take = scatter_end(chips, pairs[i], fars[i], part.at[i], got_pair.at[i], got_chip.at[i])
+        dh = take(pl.ds(0, rows))
         pair_ref[chip, core, 0, :, cols] = (dh * slope_ref[:, cols]).astype(jnp.bfloat16)
         pair_ref[chip, core, 1, :, cols] = (dh * act_ref[:, cols]).astype(jnp.bfloat16)
-    finish(sent + gather_blocks(chips, pair_ref, sems, 2 * chips))
+        gathers.append(
+            gather_start(
+                chips, pair_ref, (slice(None), slice(None), cols), sems, 4 * chips * i + 2 * chips
+            )
+        )
+        copies += list(pairs[i].values()) + fars[i]
+    for i in range(pieces):
+        cols = (slice(None), slice(None), pl.ds(i * cut, cut))
+        sent, near = gathers[i]
+        passed = gather_pass(chips, pair_ref, cols, sent, sems, 4 * chips * i + 2 * chips)
+        for copy in [near] + passed:
+            copy.wait_recv()
+        copies += sent + [near] + passed
+    finish(copies)
 
 
 def hidden_backward(chips, dy, down_weight, act, slope):
     tokens = dy.shape[0]
-    ff = down_weight.shape[0]
+    ff = down_weight.shape[1]
     rows = tokens // (2 * chips)
+    pieces = PIECES if ff % (128 * PIECES) == 0 else 1
+    cut = ff // pieces
     b16 = jnp.bfloat16
     return pl.pallas_call(
         functools.partial(hidden_kernel, chips, rows),
@@ -332,11 +396,11 @@
         in_specs=[vmem()] * 4,
         out_specs=vmem(),
         scratch_shapes=[
-            pltpu.VMEM((chips, 2, rows, ff), b16),
-            pltpu.VMEM((chips, rows, ff), b16),
-            pltpu.VMEM((chips - 1, rows, ff), b16),
-            pltpu.VMEM((chips - 1, rows, ff), b16),
-            pltpu.SemaphoreType.DMA((2, 4 * chips)),
+            pltpu.VMEM((pieces, chips, 2, rows, cut), b16),
+            pltpu.VMEM((pieces, chips, rows, cut), b16),
+            pltpu.VMEM((pieces, chips - 1, rows, cut), b16),
+            pltpu.VMEM((pieces, chips - 1, rows, cut), b16),
+            pltpu.SemaphoreType.DMA((2, 4 * chips * pieces)),
         ],
         compiler_params=pltpu.CompilerParams(
             collective_id=2, has_side_effects=True, vmem_limit_bytes=48 * 2**20
@@ -398,7 +462,7 @@
     side_ref[dp] = side[chip]
     own = pl.ds(pl.multiple_of(z * entries, 128), entries)
     logits_ref[z] = teacher_ref[:, own]
-    terms = jnp.dot(h_ref[...], down_ref[...], preferred_element_type=jnp.float32)
+    terms = contract_last(h_ref[...], down_ref[...])
     part[...] = terms.reshape(part.shape)
     down = []
     for k in range(1, depth):
@@ -478,10 +542,10 @@
 
 
 def head_kernel(
-    chips, depth, normed_ref, emb_ref, teacher_ref, factor_ref, local_ref, y_ref, side_ref,
+    chips, depth, normed_ref, emb_full, teacher_ref, factor_ref, local_ref, y_ref, side_ref,
     stats_ref, grad_emb_ref, dy_ref, back_ref,
     student, exp_s, exp_t, flat, near, dp_stats, z_stats,
-    part, got_pair, out_chip, got_chip, line_part, got_line, owned, pay, sems,
+    emb_ref, part, got_pair, out_chip, got_chip, line_part, got_line, owned, pay, sems,
 ):
     dp, z, chip, core, group, line, others, sibling = spots(chips, depth)
     count = 2 * chips
@@ -490,6 +554,9 @@
     tokens, entries = teacher_ref.shape
     f32, b16 = jnp.float32, jnp.bfloat16
     greet(group + line)
+    width = emb_full.shape[1] // count
+    for d in range(count):
+        emb_ref[d] = emb_full[:, d * width : (d + 1) * width]
     raw = contract_last(normed_ref[0], emb_ref[0])
     for d in range(1, count):
         raw += contract_last(normed_ref[d], emb_ref[d])
@@ -560,8 +627,10 @@
             ).astype(b16)
         far.append(send(out_chip.at[k - 1], got_chip.at[k - 1], sems, base + k, others[k - 1]))
     base += chips
-    for d in range(count):
-        grad_emb_ref[d] = contract_first(dlogit, normed_ref[d]).astype(b16)
+    for d in range(0, count, 2):
+        grad_emb_ref[:, d * width : (d + 2) * width] = jnp.concatenate(
+            [contract_first(dlogit, normed_ref[d + i]) for i in range(2)], axis=1
+        ).astype(b16)
     pair[0].wait_recv()
     for copy in far:
         copy.wait_recv()
@@ -611,16 +680,16 @@
     finish(first + second + list(pair.values()) + far + across + [swap] + home + last)
 
 
-def head_both(chips, depth, normed, emb_blocks, teacher, factor, local, y, side):
+def head_both(chips, depth, normed, embedding, teacher, factor, local, y, side):
     count, tokens, features = normed.shape
-    entries = emb_blocks.shape[1]
+    entries = embedding.shape[0]
     rows = y.shape[1]
     f32, b16 = jnp.float32, jnp.bfloat16
     return pl.pallas_call(
         functools.partial(head_kernel, chips, depth),
         out_shape=(
             jax.ShapeDtypeStruct((8, tokens), f32),
-            jax.ShapeDtypeStruct((count, entries, features), b16),
+            jax.ShapeDtypeStruct((entries, count * features), b16),
             jax.ShapeDtypeStruct((chips, depth, rows, features), b16),
             jax.ShapeDtypeStruct((chips, 2, rows, features), b16),
         ),
@@ -634,6 +703,7 @@
             pltpu.VMEM((8, tokens), f32),
             pltpu.VMEM((count, 8, tokens), f32),
             pltpu.VMEM((depth, 8, tokens), f32),
+            pltpu.VMEM((count, entries, features), b16),
             pltpu.VMEM((count, chips, depth, rows, features), b16),
             pltpu.VMEM((chips, chips, depth, rows, features), b16),
             pltpu.VMEM((chips - 1, chips, depth, rows, features), b16),
@@ -647,7 +717,7 @@
         compiler_params=pltpu.CompilerParams(
             collective_id=4, has_side_effects=True, vmem_limit_bytes=48 * 2**20
         ),
-    )(normed, emb_blocks, teacher, factor, local, y, side)
+    )(normed, embedding, teacher, factor, local, y, side)
 
 
 def input_kernel(
@@ -749,18 +819,17 @@
     x_blocks = hidden_in.reshape(chips, depth, rows, features)
     gains = jnp.pad(jnp.stack([post_gain, final_gain]), ((0, 6), (0, 0)))
     normed, y, side, teacher = branch_forward(
-        chips, depth, hidden, down_weight, x_blocks, gains, teacher_logits
+        chips, depth, hidden, down_weight.T, x_blocks, gains, teacher_logits
     )
     entries = embedding.shape[0]
     mask = token_mask(lengths, positions)
     count = jnp.sum(lengths).astype(jnp.float32)
     first_entry = lax.axis_index(("dp", "vocab")) * entries
-    emb_blocks = embedding.reshape(entries, 2 * chips, features).transpose(1, 0, 2)
     stats, grad_emb, dy_blocks, back = head_both(
         chips,
         depth,
         normed.reshape(2 * chips, positions, features),
-        emb_blocks,
+        embedding,
         teacher.reshape(positions, entries),
         (loss_scale / count * mask)[:, None],
         (target_ids - first_entry)[:, None],
@@ -772,9 +841,9 @@
     log_t = jnp.log(total_t)
     per_token = weighted / total_t - log_t + log_s + hard_weight * (log_s - picked)
     loss = jnp.sum(mask * per_token) / count
-    grad_embedding = grad_emb.transpose(1, 0, 2).reshape(entries, -1)
+    grad_embedding = grad_emb
     grad_out = dy_blocks.reshape(positions, features)
-    pairs = hidden_backward(chips, grad_out, down_weight, act, slope)
+    pairs = hidden_backward(chips, grad_out, down_weight.T, act, slope)
     dgate = pairs[:, :, 0].reshape(positions, -1)
     dup = pairs[:, :, 1].reshape(positions, -1)
     grad_down = contract_first(hidden, grad_out).astype(jnp.bfloat16)

time: 255 us -> 228 us (0.89)
  local copies, waits for them, and re-layouts: 29.7 us -> 9.9 us
  Pallas kernels: 209 us -> 200 us
  other arithmetic: 2.23 us -> 4.92 us
    unnamed x43 -> x21, local copies, waits for them, and re-layouts: 22.8 us -> 6.48 us
    pallas_call x1, Pallas kernels: 50.4 us -> 43.3 us  [ffn_forward(): pl.pallas_call(functools.partial(ffn_kernel, chips, rows), out_shape=(jax...]
    reshape x1 -> x0, local copies, waits for them, and re-layouts: 3.89 us -> none  [on_device(): embedding.reshape(entries, 2 * chips, features).transpose(1, 0, 2)]
    pallas_call x1, Pallas kernels: 41.4 us -> 38.7 us  [hidden_backward(): pl.pallas_call(functools.partial(hidden_kernel, chips, rows), out_shape=j...]
where the time goes in v3:
time: 228 us
  Pallas kernels  200 us (88%)
  local copies, waits for them, and re-layouts  9.9 us (4%)
  matrix products  9.65 us (4%)
  other arithmetic  4.92 us (2%)
  between operations  3.28 us (1%)
    pallas_call x1, Pallas kernels, head_both(): pl.pallas_call(functools.partial(head_kernel, chips, depth), out_shape=(j...  47.6 us
    pallas_call x1, Pallas kernels, branch_forward(): pl.pallas_call(functools.partial(branch_kernel, chips, depth), out_shape=...  43.7 us
    pallas_call x1, Pallas kernels, ffn_forward(): pl.pallas_call(functools.partial(ffn_kernel, chips, rows), out_shape=(jax...  43.3 us
    pallas_call x1, Pallas kernels, hidden_backward(): pl.pallas_call(functools.partial(hidden_kernel, chips, rows), out_shape=j...  38.7 us
    pallas_call x1, Pallas kernels, input_backward(): pl.pallas_call(functools.partial(input_kernel, chips, depth), out_shape=j...  26.6 us
    dot_general x3, matrix products, contract_first(): lax.dot_general(left, right, (((0,), (0,)), ((), ())), preferred_element_...  9.65 us
    unnamed x21, local copies, waits for them, and re-layouts  6.48 us

profile of v3, /device:TPU:0, one launch (start us, length us, event | category | flops | bytes accessed | tf_op | source)
XLA Modules:
  0.0 227.7 jit_solution(8678487925610185760)
XLA Ops:
  0.6 1.3 reduce_sum.40
  2.6 0.7 broadcast_subtract_fusion
  3.3 0.7 fusion.6
  4.1 0.7 select_maximum_fusion.gains_ref
  4.8 0.7 broadcast_in_dim.52.gain_ref
  5.5 0.1 copy.28.local_ref
  5.6 0.1 copy.27
  5.8 1.1 copy.25
  6.9 0.8 fusion.1
  7.7 0.1 broadcast_in_dim.48.square_ref
  7.8 0.0 copy-start.8
  7.8 43.3 %shard_map.154 = (bf16[4,2,32,3584]{3,2,1,0:T(8,128)(2,1)S(1)}, f32[32,3584]{1,0:T(8,128)S(1)}, f32[32,3584]{1,0:T(8,128)S(1)}) custom-call(bf16[256,448]{1,0:T(8,128)(2,1)S(1)} %get-tuple-element.49.x_ref, f32[256,128]{1,0:T(8,128)S(1)} %broadcast_in_dim.48.square_ref, bf16[448,3584]{1,0:T(8,128)(2,1)} %gate_ref.3, bf16[448,3584]{1,0:T(8,128)(2,1)} %up_ref.3), custom_call_target="tpu_custom_call" | custom-call | tf_op jit(solution)/shard_map/pallas_call | solution.py:311
  51.2 0.0 copy-start.6
  51.2 0.8 copy-done.6
  51.9 0.0 copy-done.8
  51.9 0.0 copy-start.5
  51.9 43.7 %shard_map.155 = (bf16[8,4,4,16,448]{4,3,2,1,0:T(8,128)(2,1)S(1)}, f32[8,16,448]{2,1,0:T(8,128)S(1)}, f32[8,24,448]{2,1,0:T(8,128)S(1)}, bf16[4,64,256]{2,1,0:T(8,128)(2,1)S(1)}) custom-call(bf16[256,3584]{1,0:T(8,128)(2,1)S(1)} %bitcast.26, bf16[448,3584]{1,0:T(8,128)(2,1)} %bitcast.24, bf16[4,4,16,448]{3,2,1,0:T(8,128)(2,1)S(1)} %bitcast.28, ...), custom_call_target="tpu_custom_call" | custom-call | tf_op jit(solution)/shard_map/pallas_call | solution.py:521
  95.7 0.0 copy-start.2
  95.7 1.3 copy-done.2
  97.0 0.0 copy-done.5
  97.0 47.6 %shard_map.156 = (f32[8,256]{1,0:T(8,128)S(1)}, bf16[256,3584]{1,0:T(8,128)(2,1)S(1)}, bf16[4,4,16,448]{3,2,1,0:T(8,128)(2,1)S(1)}, bf16[4,2,16,448]{3,2,1,0:T(8,128)(2,1)S(1)}) custom-call(bf16[8,256,448]{2,1,0:T(8,128)(2,1)} %bitcast.30, bf16[256,3584]{1,0:T(8,128)(2,1)S(1)} %copy-done.5, bf16[256,256]{1,0:T(8,128)(2,1)S(1)} %bitcast.34, ...), custom_call_target="tpu_custom_call" | custom-call | tf_op jit(solution)/shard_map/pallas_call | solution.py:688
  144.6 0.0 copy-start.3
  144.6 1.2 copy-done.3
  145.8 0.6 fusion.9
  147.1 0.0 copy-start.1
  147.1 0.0 copy-start.7
  147.1 2.7 %convolution_convert_fusion = bf16[3584,448]{0,1:T(8,128)(2,1)} fusion(bf16[256,3584]{1,0:T(8,128)(2,1)S(1)} %bitcast.27, bf16[256,448]{1,0:T(8,128)(2,1)S(1)} %bitcast.31), kind=kOutput, calls=%fused_computation | convolution fusion | flops 823689216 | bytes 5275648 | tf_op jit(solution)/shard_map/dot_general | solution.py:39
  149.9 0.0 copy-done.1
  149.9 0.0 copy-done.7
  149.9 38.7 %shard_map.157 = bf16[4,2,2,32,3584]{4,3,2,1,0:T(8,128)(2,1)} custom-call(bf16[256,448]{1,0:T(8,128)(2,1)S(1)} %bitcast.32, bf16[448,3584]{1,0:T(8,128)(2,1)S(1)} %bitcast.25, f32[32,3584]{1,0:T(8,128)S(1)} %get-tuple-element.24.act_ref, f32[32,3584]{1,0:T(8,128)S(1)} %copy-done.7), custom_call_target="tpu_custom_call" | custom-call | tf_op jit(solution)/shard_map/pallas_call | solution.py:393
  188.6 2.4 %fusion.10 = (bf16[4,2,1,32,3584]{4,3,2,1,0:T(8,128)(2,1)S(1)}, bf16[4,2,1,32,3584]{4,3,2,1,0:T(8,128)(2,1)S(1)}) fusion(bf16[4,2,2,32,3584]{4,3,2,1,0:T(8,128)(2,1)} %shard_map.157), kind=kLoop, calls=%fused_computation.29 | loop fusion | bytes 7340032 | tf_op jit(solution)/shard_map/slice | solution.py:848
  191.0 0.0 copy-start
  191.0 26.6 %shard_map.158 = bf16[4,4,16,448]{3,2,1,0:T(8,128)(2,1)S(1)} custom-call(bf16[256,3584]{1,0:T(8,128)(2,1)S(1)} %bitcast.20, bf16[256,3584]{1,0:T(8,128)(2,1)S(1)} %bitcast.22, bf16[448,3584]{1,0:T(8,128)(2,1)} %gate_ref.3, bf16[448,3584]{1,0:T(8,128)(2,1)} %up_ref.3, bf16[4,4,16,448]{3,2,1,0:T(8,128)(2,1)S(1)} %bitcast.29, ...), custom_call_target="tpu_custom_call" | custom-call | tf_op jit(solution)/shard_map/pallas_call | solution.py:772
  217.6 0.0 copy-done
  217.6 0.8 copy.29
  218.4 4.2 %convolution_convert_fusion.1 = bf16[448,3584]{1,0:T(8,128)(2,1)} fusion(bf16[256,448]{1,0:T(8,128)(2,1)S(1)} %get-tuple-element.49.x_ref, bf16[256,3584]{1,0:T(8,128)(2,1)} %bitcast.23), kind=kOutput, calls=%fused_computation.1 | convolution fusion | flops 823689216 | bytes 5275648 | tf_op jit(solution)/shard_map/dot_general | solution.py:39
  222.6 0.0 copy-start.4
  222.6 2.7 %convolution_convert_fusion.2 = bf16[448,3584]{1,0:T(8,128)(2,1)} fusion(bf16[256,448]{1,0:T(8,128)(2,1)S(1)} %get-tuple-element.49.x_ref, bf16[256,3584]{1,0:T(8,128)(2,1)S(1)} %bitcast.21), kind=kOutput, calls=%fused_computation.2 | convolution fusion | flops 823689216 | bytes 5275648 | tf_op jit(solution)/shard_map/dot_general | solution.py:39
  225.3 0.0 copy-done.4
  225.3 1.2 copy.31
  (3 shorter events, 0.0 us)
Async XLA Ops:
  7.8 44.1 %copy-start.8 = (bf16[64,1024]{1,0:T(8,128)(2,1)S(1)}, bf16[64,1024]{1,0:T(8,128)(2,1)}, u32[]{:S(2)}) copy-start(bf16[64,1024]{1,0:T(8,128)(2,1)} %teacher_ref.1) | copy-start | bytes 393220
  51.2 0.8 copy-start.6
  51.9 45.1 %copy-start.5 = (bf16[256,3584]{1,0:T(8,128)(2,1)S(1)}, bf16[256,3584]{1,0:T(8,128)(2,1)}, u32[]{:S(2)}) copy-start(bf16[256,3584]{1,0:T(8,128)(2,1)} %emb_full.1) | copy-start | bytes 5505028
  95.7 1.3 copy-start.2
  144.6 1.2 copy-start.3
  147.1 2.8 %copy-start.1 = (bf16[3584,448]{0,1:T(8,128)(2,1)S(1)}, bf16[3584,448]{0,1:T(8,128)(2,1)}, u32[]{:S(2)}) copy-start(bf16[3584,448]{0,1:T(8,128)(2,1)} %param.15) | copy-start | bytes 9633796
  147.1 2.7 %copy-start.7 = (f32[32,3584]{1,0:T(8,128)S(1)}, f32[32,3584]{1,0:T(8,128)}, u32[]{:S(2)}) copy-start(f32[32,3584]{1,0:T(8,128)} %copy-done.6) | copy-start | bytes 1376260
  191.0 26.6 %copy-start = (bf16[4,2,1,32,3584]{4,3,2,1,0:T(8,128)(2,1)}, bf16[4,2,1,32,3584]{4,3,2,1,0:T(8,128)(2,1)S(1)}, u32[]{:S(2)}) copy-start(bf16[4,2,1,32,3584]{4,3,2,1,0:T(8,128)(2,1)S(1)} %get-tuple-element.46) | copy-start | bytes 5505028
  222.6 2.7 %copy-start.4 = (bf16[256,3584]{1,0:T(8,128)(2,1)S(1)}, bf16[256,3584]{1,0:T(8,128)(2,1)}, u32[]{:S(2)}) copy-start(bf16[256,3584]{1,0:T(8,128)(2,1)} %copy-done.3) | copy-start | bytes 5505028

commit v4 on v3

--- a/solution.py
+++ b/solution.py
@@ -463,7 +463,7 @@
     own = pl.ds(pl.multiple_of(z * entries, 128), entries)
     logits_ref[z] = teacher_ref[:, own]
     terms = contract_last(h_ref[...], down_ref[...])
-    part[...] = terms.reshape(part.shape)
+    part[...] = terms.astype(jnp.bfloat16).reshape(part.shape)
     down = []
     for k in range(1, depth):
         there = lax.rem(z + k, depth)
@@ -471,9 +471,9 @@
     base += depth
     for copy in down:
         copy.wait_recv()
-    summed = part[:, z]
-    for k in range(1, depth):
-        summed += got[k - 1]
+    summed = part[:, z].astype(jnp.float32)
+    for k in range(1, depth):
+        summed += got[k - 1].astype(jnp.float32)
     total[...] = summed
     across = []
     for k in range(1, count):
@@ -530,8 +530,8 @@
         out_specs=(vmem(),) * 4,
         scratch_shapes=[
             pltpu.VMEM((chips, rows + 8, features), f32),
-            pltpu.VMEM((chips, depth, rows, features), f32),
-            pltpu.VMEM((depth - 1, chips, rows, features), f32),
+            pltpu.VMEM((chips, depth, rows, features), jnp.bfloat16),
+            pltpu.VMEM((depth - 1, chips, rows, features), jnp.bfloat16),
             pltpu.VMEM((chips, rows, features), f32),
             pltpu.SemaphoreType.DMA((2, 4 * depth + 5 * chips + chips * depth)),
         ],

time: 228 us -> 222 us (0.974)
  Pallas kernels: 200 us -> 194 us
    pallas_call x1, Pallas kernels: 43.7 us -> 38.1 us  [branch_forward(): pl.pallas_call(functools.partial(branch_kernel, chips, depth), out_shape=...]
where the time goes in v4:
time: 222 us
  Pallas kernels  194 us (87%)
  local copies, waits for them, and re-layouts  9.9 us (4%)
  matrix products  9.65 us (4%)
  other arithmetic  4.92 us (2%)
  between operations  3.28 us (1%)
    pallas_call x1, Pallas kernels, head_both(): pl.pallas_call(functools.partial(head_kernel, chips, depth), out_shape=(j...  47.2 us
    pallas_call x1, Pallas kernels, ffn_forward(): pl.pallas_call(functools.partial(ffn_kernel, chips, rows), out_shape=(jax...  43.3 us
    pallas_call x1, Pallas kernels, hidden_backward(): pl.pallas_call(functools.partial(hidden_kernel, chips, rows), out_shape=j...  39.1 us
    pallas_call x1, Pallas kernels, branch_forward(): pl.pallas_call(functools.partial(branch_kernel, chips, depth), out_shape=...  38.1 us
    pallas_call x1, Pallas kernels, input_backward(): pl.pallas_call(functools.partial(input_kernel, chips, depth), out_shape=j...  26.6 us
    dot_general x3, matrix products, contract_first(): lax.dot_general(left, right, (((0,), (0,)), ((), ())), preferred_element_...  9.65 us
    unnamed x21, local copies, waits for them, and re-layouts  6.48 us

profile of v4, /device:TPU:0, one launch (start us, length us, event | category | flops | bytes accessed | tf_op | source)
XLA Modules:
  0.0 222.1 jit_solution(10760043722980641204)
XLA Ops:
  0.6 1.3 reduce_sum.40
  2.6 0.7 broadcast_subtract_fusion
  3.3 0.7 fusion.6
  4.1 0.7 select_maximum_fusion.gains_ref
  4.8 0.7 broadcast_in_dim.52.gain_ref
  5.5 0.1 copy.28.local_ref
  5.6 0.1 copy.27
  5.8 1.1 copy.25
  6.9 0.8 fusion.1
  7.7 0.1 broadcast_in_dim.48.square_ref
  7.8 0.0 copy-start.8
  7.8 43.3 %shard_map.154 = (bf16[4,2,32,3584]{3,2,1,0:T(8,128)(2,1)S(1)}, f32[32,3584]{1,0:T(8,128)S(1)}, f32[32,3584]{1,0:T(8,128)S(1)}) custom-call(bf16[256,448]{1,0:T(8,128)(2,1)S(1)} %get-tuple-element.49.x_ref, f32[256,128]{1,0:T(8,128)S(1)} %broadcast_in_dim.48.square_ref, bf16[448,3584]{1,0:T(8,128)(2,1)} %gate_ref.3, bf16[448,3584]{1,0:T(8,128)(2,1)} %up_ref.3), custom_call_target="tpu_custom_call" | custom-call | tf_op jit(solution)/shard_map/pallas_call | solution.py:311
  51.2 0.0 copy-start.6
  51.2 0.8 copy-done.6
  51.9 0.0 copy-done.8
  51.9 0.0 copy-start.5
  51.9 38.1 %shard_map.155 = (bf16[8,4,4,16,448]{4,3,2,1,0:T(8,128)(2,1)S(1)}, f32[8,16,448]{2,1,0:T(8,128)S(1)}, f32[8,24,448]{2,1,0:T(8,128)S(1)}, bf16[4,64,256]{2,1,0:T(8,128)(2,1)S(1)}) custom-call(bf16[256,3584]{1,0:T(8,128)(2,1)S(1)} %bitcast.26, bf16[448,3584]{1,0:T(8,128)(2,1)} %bitcast.24, bf16[4,4,16,448]{3,2,1,0:T(8,128)(2,1)S(1)} %bitcast.28, ...), custom_call_target="tpu_custom_call" | custom-call | tf_op jit(solution)/shard_map/pallas_call | solution.py:521
  90.1 0.0 copy-start.2
  90.1 1.3 copy-done.2
  91.4 0.0 copy-done.5
  91.4 47.2 %shard_map.156 = (f32[8,256]{1,0:T(8,128)S(1)}, bf16[256,3584]{1,0:T(8,128)(2,1)S(1)}, bf16[4,4,16,448]{3,2,1,0:T(8,128)(2,1)S(1)}, bf16[4,2,16,448]{3,2,1,0:T(8,128)(2,1)S(1)}) custom-call(bf16[8,256,448]{2,1,0:T(8,128)(2,1)} %bitcast.30, bf16[256,3584]{1,0:T(8,128)(2,1)S(1)} %copy-done.5, bf16[256,256]{1,0:T(8,128)(2,1)S(1)} %bitcast.34, ...), custom_call_target="tpu_custom_call" | custom-call | tf_op jit(solution)/shard_map/pallas_call | solution.py:688
  138.6 0.0 copy-start.3
  138.7 1.2 copy-done.3
  139.9 0.6 fusion.9
  141.2 0.0 copy-start.1
  141.2 0.0 copy-start.7
  141.2 2.7 %convolution_convert_fusion = bf16[3584,448]{0,1:T(8,128)(2,1)} fusion(bf16[256,3584]{1,0:T(8,128)(2,1)S(1)} %bitcast.27, bf16[256,448]{1,0:T(8,128)(2,1)S(1)} %bitcast.31), kind=kOutput, calls=%fused_computation | convolution fusion | flops 823689216 | bytes 5275648 | tf_op jit(solution)/shard_map/dot_general | solution.py:39
  143.9 0.0 copy-done.1
  143.9 0.0 copy-done.7
  143.9 39.1 %shard_map.157 = bf16[4,2,2,32,3584]{4,3,2,1,0:T(8,128)(2,1)} custom-call(bf16[256,448]{1,0:T(8,128)(2,1)S(1)} %bitcast.32, bf16[448,3584]{1,0:T(8,128)(2,1)S(1)} %bitcast.25, f32[32,3584]{1,0:T(8,128)S(1)} %get-tuple-element.24.act_ref, f32[32,3584]{1,0:T(8,128)S(1)} %copy-done.7), custom_call_target="tpu_custom_call" | custom-call | tf_op jit(solution)/shard_map/pallas_call | solution.py:393
  183.0 2.4 %fusion.10 = (bf16[4,2,1,32,3584]{4,3,2,1,0:T(8,128)(2,1)S(1)}, bf16[4,2,1,32,3584]{4,3,2,1,0:T(8,128)(2,1)S(1)}) fusion(bf16[4,2,2,32,3584]{4,3,2,1,0:T(8,128)(2,1)} %shard_map.157), kind=kLoop, calls=%fused_computation.29 | loop fusion | bytes 7340032 | tf_op jit(solution)/shard_map/slice | solution.py:848
  185.4 0.0 copy-start
  185.4 26.6 %shard_map.158 = bf16[4,4,16,448]{3,2,1,0:T(8,128)(2,1)S(1)} custom-call(bf16[256,3584]{1,0:T(8,128)(2,1)S(1)} %bitcast.20, bf16[256,3584]{1,0:T(8,128)(2,1)S(1)} %bitcast.22, bf16[448,3584]{1,0:T(8,128)(2,1)} %gate_ref.3, bf16[448,3584]{1,0:T(8,128)(2,1)} %up_ref.3, bf16[4,4,16,448]{3,2,1,0:T(8,128)(2,1)S(1)} %bitcast.29, ...), custom_call_target="tpu_custom_call" | custom-call | tf_op jit(solution)/shard_map/pallas_call | solution.py:772
  212.0 0.0 copy-done
  212.0 0.8 copy.29
  212.8 4.2 %convolution_convert_fusion.1 = bf16[448,3584]{1,0:T(8,128)(2,1)} fusion(bf16[256,448]{1,0:T(8,128)(2,1)S(1)} %get-tuple-element.49.x_ref, bf16[256,3584]{1,0:T(8,128)(2,1)} %bitcast.23), kind=kOutput, calls=%fused_computation.1 | convolution fusion | flops 823689216 | bytes 5275648 | tf_op jit(solution)/shard_map/dot_general | solution.py:39
  217.0 0.0 copy-start.4
  217.0 2.7 %convolution_convert_fusion.2 = bf16[448,3584]{1,0:T(8,128)(2,1)} fusion(bf16[256,448]{1,0:T(8,128)(2,1)S(1)} %get-tuple-element.49.x_ref, bf16[256,3584]{1,0:T(8,128)(2,1)S(1)} %bitcast.21), kind=kOutput, calls=%fused_computation.2 | convolution fusion | flops 823689216 | bytes 5275648 | tf_op jit(solution)/shard_map/dot_general | solution.py:39
  219.7 0.0 copy-done.4
  219.7 1.2 copy.31
  (3 shorter events, 0.0 us)
Async XLA Ops:
  7.8 44.1 %copy-start.8 = (bf16[64,1024]{1,0:T(8,128)(2,1)S(1)}, bf16[64,1024]{1,0:T(8,128)(2,1)}, u32[]{:S(2)}) copy-start(bf16[64,1024]{1,0:T(8,128)(2,1)} %teacher_ref.1) | copy-start | bytes 393220
  51.2 0.8 copy-start.6
  51.9 39.5 %copy-start.5 = (bf16[256,3584]{1,0:T(8,128)(2,1)S(1)}, bf16[256,3584]{1,0:T(8,128)(2,1)}, u32[]{:S(2)}) copy-start(bf16[256,3584]{1,0:T(8,128)(2,1)} %emb_full.1) | copy-start | bytes 5505028
  90.1 1.3 copy-start.2
  138.6 1.2 copy-start.3
  141.2 2.8 %copy-start.1 = (bf16[3584,448]{0,1:T(8,128)(2,1)S(1)}, bf16[3584,448]{0,1:T(8,128)(2,1)}, u32[]{:S(2)}) copy-start(bf16[3584,448]{0,1:T(8,128)(2,1)} %param.15) | copy-start | bytes 9633796
  141.2 2.8 %copy-start.7 = (f32[32,3584]{1,0:T(8,128)S(1)}, f32[32,3584]{1,0:T(8,128)}, u32[]{:S(2)}) copy-start(f32[32,3584]{1,0:T(8,128)} %copy-done.6) | copy-start | bytes 1376260
  185.4 26.6 %copy-start = (bf16[4,2,1,32,3584]{4,3,2,1,0:T(8,128)(2,1)}, bf16[4,2,1,32,3584]{4,3,2,1,0:T(8,128)(2,1)S(1)}, u32[]{:S(2)}) copy-start(bf16[4,2,1,32,3584]{4,3,2,1,0:T(8,128)(2,1)S(1)} %get-tuple-element.46) | copy-start | bytes 5505028
  217.0 2.7 %copy-start.4 = (bf16[256,3584]{1,0:T(8,128)(2,1)S(1)}, bf16[256,3584]{1,0:T(8,128)(2,1)}, u32[]{:S(2)}) copy-start(bf16[256,3584]{1,0:T(8,128)(2,1)} %copy-done.3) | copy-start | bytes 5505028
